TPU v7x, 256 devices: a whole 4x4x8 slice. The times are simulated.
256 devices in a mesh: replica: 16 (over y_lo, z), fsdp: 16 (over y_hi, x, core).
Axes of the slice: x: 4, y: 4 (y_hi: 2, y_lo: 2; y = y_hi * 2 + y_lo), z: 8, core: 2. Of those that a mesh axis runs over, the one named last changes fastest.
Arguments:
- hidden: bfloat16 [16, 4096, 4096], P('replica', 'fsdp'), may hold values from -6 to 6
- key_weight: bfloat16 [16, 4096, 1024], P('replica', 'fsdp'), may hold values from -0.09375 to 0.09375
- adam_first: float32 [16, 4096, 1024], P('replica', 'fsdp'), may hold values from -120 to 120
- adam_second: float32 [16, 4096, 1024], P('replica', 'fsdp'), may hold values from 100 to 4000
- key_cotangent: bfloat16 [16, 4096, 1024], P('replica', 'fsdp'), may hold values from -6 to 6
- frag_global: float32 [4096, 1024], P('fsdp'), may hold values from -6 to 6
- frag_momentum: float32 [4096, 1024], P('fsdp'), may hold values from -3 to 3
- frag_local: bfloat16 [16, 4096, 1024], P('replica', 'fsdp'), may hold values from -6 to 6
Outputs:
- keys: bfloat16 [16, 4096, 1024], P('replica', 'fsdp')
- input_grad: bfloat16 [16, 4096, 4096], P('replica', 'fsdp')
- new_weight: bfloat16 [16, 4096, 1024], P('replica', 'fsdp')
- new_first: float32 [16, 4096, 1024], P('replica', 'fsdp')
- new_second: float32 [16, 4096, 1024], P('replica', 'fsdp')
- new_global: float32 [4096, 1024], P('fsdp')
- new_momentum: float32 [4096, 1024], P('fsdp')
All inputs are finite; a program needn't handle non-finite values.
Results may differ from a plain program's by a relative error of at most 0.011.
Values may be sent and summed in bfloat16 or wider, within the bound.
No kernel may reach another device: no remote copies, remote signals or barrier semaphores. Data moves between devices by JAX's collectives and lax.ppermute only.
A program may use at most 128 MiB of HBM per device.

v0:
```python
import jax
import jax.numpy as jnp
from jax import lax
from jax.sharding import PartitionSpec as P

first_bias = 0.9999734386011124
second_bias = 0.9940794707796655


def body(
    hidden,
    key_weight,
    adam_first,
    adam_second,
    key_cotangent,
    frag_global,
    frag_momentum,
    frag_local,
):
    inputs = hidden[0]
    weight = key_weight[0]
    cotangent = key_cotangent[0]
    islands = lax.axis_size("replica")
    pseudo_terms = frag_global - frag_local[0].astype(jnp.float32)
    summed = lax.psum(pseudo_terms, "replica")
    pseudo = summed / islands
    new_momentum = 0.9 * frag_momentum + pseudo
    new_global = frag_global - 0.7 * (pseudo + 0.9 * new_momentum)
    whole = lax.all_gather(weight, "fsdp", axis=0, tiled=True)
    keys = jnp.dot(inputs, whole, preferred_element_type=jnp.float32).astype(jnp.bfloat16)
    input_grad = lax.dot_general(
        cotangent, whole, (((1,), (1,)), ((), ())), preferred_element_type=jnp.float32
    ).astype(jnp.bfloat16)
    grad = lax.psum_scatter(
        lax.dot_general(
            inputs, cotangent, (((0,), (0,)), ((), ())), preferred_element_type=jnp.float32
        ).astype(jnp.bfloat16),
        "fsdp",
        scatter_dimension=0,
        tiled=True,
    ).astype(jnp.float32)
    new_first = 0.9 * adam_first[0] + 0.1 * grad
    new_second = 0.95 * adam_second[0] + 0.05 * grad * grad
    update = new_first / first_bias / (jnp.sqrt(new_second / second_bias) + 1e-08)
    old_weight = weight.astype(jnp.float32)
    new_weight = (old_weight - 0.003 * (update + 0.1 * old_weight)).astype(jnp.bfloat16)
    return (
        keys[None],
        input_grad[None],
        new_weight[None],
        new_first[None],
        new_second[None],
        new_global,
        new_momentum,
    )


def solution(mesh):
    return jax.shard_map(
        body,
        mesh=mesh,
        in_specs=(
            P("replica", "fsdp", None),
            P("replica", "fsdp", None),
            P("replica", "fsdp", None),
            P("replica", "fsdp", None),
            P("replica", "fsdp", None),
            P("fsdp", None),
            P("fsdp", None),
            P("replica", "fsdp", None),
        ),
        out_specs=(
            P("replica", "fsdp", None),
            P("replica", "fsdp", None),
            P("replica", "fsdp", None),
            P("replica", "fsdp", None),
            P("replica", "fsdp", None),
            P("fsdp", None),
            P("fsdp", None),
        ),
        check_vma=False,
    )
```

profile of v0, /device:TPU:6, one launch (start us, length us, event | category | flops | bytes accessed | tf_op | source)
XLA Modules:
  0.0 227.5 jit_solution(15138089796335735515)
XLA Ops:
  8.0 0.0 copy-start
  8.0 0.0 all-reduce.2.cloned.1.call-start
  8.1 2.7 %convert_subtract_fusion.1 = f32[256,1024]{1,0:T(8,128)} fusion(f32[256,1024]{1,0:T(8,128)} %param.13, bf16[1,256,1024]{2,1,0:T(8,128)(2,1)} %param.15), kind=kLoop, calls=%fused_computation.20 | loop fusion | flops 524288 | bytes 2621440 | tf_op jit(solution)/shard_map/sub | solution.py:24
  10.7 0.0 all-reduce.2.cloned.1.call-update
  10.7 0.0 copy-start.1
  10.8 0.0 reduce-scatter.2.cloned.1.call-start
  10.8 0.0 copy-done
  10.8 6.7 %convolution_convert_fusion = bf16[4096,1024]{1,0:T(8,128)(2,1)} fusion(bf16[1,256,4096]{2,1,0:T(8,128)(2,1)S(1)} %copy-done, bf16[1,256,1024]{2,1,0:T(8,128)(2,1)} %param.12), kind=kOutput, calls=%fused_computation.4 | convolution fusion | flops 2151677952 | bytes 11010048 | tf_op jit(solution)/shard_map/dot_general | solution.py:35
  17.6 0.0 reduce-scatter.2.cloned.1.call-update
  17.6 0.0 all-gather.3.cloned.1.call-start
  17.6 0.5 all-gather.3.cloned.1.call-update
  18.2 134.7 %all-reduce.2.cloned.1.call-done = f32[256,1024]{1,0:T(8,128)} async-done(((f32[256,1024]{1,0:T(8,128)}), f32[256,1024]{1,0:T(8,128)}) %all-reduce.2.cloned.1.call-update) | async-done | bytes 1048592 | tf_op jit(solution)/shard_map/psum | solution.py:25
  152.8 0.0 copy-done.1
  152.8 3.3 %multiply_subtract_fusion = (f32[256,1024]{1,0:T(8,128)}, f32[256,1024]{1,0:T(8,128)}) fusion(f32[256,1024]{1,0:T(8,128)S(1)} %copy-done.1, f32[256,1024]{1,0:T(8,128)} %all-reduce.2.cloned.1.call-done, f32[256,1024]{1,0:T(8,128)} %param.14), kind=kLoop, calls=%fused_computation.21 | loop fusion | flops 1835008 | bytes 5242880 | tf_op jit(solution)/shard_map/sub | solution.py:28
  156.2 0.0 reduce-scatter.2.cloned.1.call-done
  156.2 4.2 %fusion.28 = (f32[1,256,1024]{2,1,0:T(8,128)}, bf16[1,256,1024]{2,1,0:T(8,128)(2,1)}, f32[1,256,1024]{2,1,0:T(8,128)}) fusion(bf16[256,1024]{1,0:T(8,128)(2,1)} %reduce-scatter.2.cloned.1.call-done, f32[1,256,1024]{2,1,0:T(8,128)} %param.11, f32[1,256,1024]{2,1,0:T(8,128)} %param.10, bf16[1,256,1024]{2,1,0:T(8,128)(2,1)} %param.9), kind=kLoop, calls=%fused_computation.24 | loop fusion | flops 4718592 | bytes 5767168 | tf_op jit(solution)/shard_map/broadcast_in_dim | solution.py:52
  160.4 0.0 copy-start.2
  160.4 49.2 %all-gather.3.cloned.1.call-done = bf16[1,4096,1024]{2,1,0:T(8,128)(2,1)} async-done(((bf16[1,256,1024]{2,1,0:T(8,128)(2,1)}), bf16[1,4096,1024]{2,1,0:T(8,128)(2,1)}) %all-gather.3.cloned.1.call-update) | async-done | bytes 8388624 | tf_op jit(solution)/shard_map/all_gather | solution.py:29
  209.6 0.0 copy-start.3
  209.6 6.7 %fusion.17 = bf16[1,256,1024]{2,1,0:T(8,128)(2,1)} fusion(bf16[1,4096,1024]{2,1,0:T(8,128)(2,1)} %all-gather.3.cloned.1.call-done, bf16[1,256,4096]{2,1,0:T(8,128)(2,1)S(1)} %copy-done), kind=kOutput, calls=%fused_computation.14 | convolution fusion | flops 2147745792 | bytes 11010048 | tf_op jit(solution)/shard_map/dot_general | solution.py:30
  216.3 0.0 copy-done.2
  216.3 0.0 copy-done.3
  216.3 3.8 %fusion.7 = bf16[1,256,4096]{2,1,0:T(8,128)(2,1)} fusion(bf16[1,4096,1024]{2,1,0:T(8,128)(2,1)S(1)} %copy-done.3, bf16[1,256,1024]{2,1,0:T(8,128)(2,1)S(1)} %copy-done.2), kind=kOutput, calls=%fused_computation.6 | convolution fusion | flops 2148532224 | bytes 11010048 | tf_op jit(solution)/shard_map/dot_general | solution.py:31
Async XLA Ops:
  8.0 2.8 %copy-start = (bf16[1,256,4096]{2,1,0:T(8,128)(2,1)S(1)}, bf16[1,256,4096]{2,1,0:T(8,128)(2,1)}, u32[]{:S(2)}) copy-start(bf16[1,256,4096]{2,1,0:T(8,128)(2,1)} %param.8) | copy-start | bytes 6291460
  8.0 144.8 %all-reduce.2.cloned.1.call-start = ((), (), s32[]{:S(2)}) async-start(), calls=%async_computation.2 | async-start | bytes 2097152 | tf_op jit(solution)/shard_map/psum | solution.py:25
  10.7 142.1 %copy-start.1 = (f32[256,1024]{1,0:T(8,128)S(1)}, f32[256,1024]{1,0:T(8,128)}, u32[]{:S(2)}) copy-start(f32[256,1024]{1,0:T(8,128)} %param.13) | copy-start | bytes 3145732
  10.8 145.4 %reduce-scatter.2.cloned.1.call-start = ((), (), s32[]{:S(2)}) async-start(), calls=%async_computation.1 | async-start | bytes 8912896 | tf_op jit(solution)/shard_map/reduce_scatter | solution.py:34
  17.6 192.0 %all-gather.3.cloned.1.call-start = ((), (), s32[]{:S(2)}) async-start(), calls=%async_computation.3 | async-start | bytes 8912896 | tf_op jit(solution)/shard_map/all_gather | solution.py:29
  160.4 55.9 %copy-start.2 = (bf16[1,256,1024]{2,1,0:T(8,128)(2,1)S(1)}, bf16[1,256,1024]{2,1,0:T(8,128)(2,1)}, u32[]{:S(2)}) copy-start(bf16[1,256,1024]{2,1,0:T(8,128)(2,1)} %param.12) | copy-start | bytes 1572868
  209.6 6.7 %copy-start.3 = (bf16[1,4096,1024]{2,1,0:T(8,128)(2,1)S(1)}, bf16[1,4096,1024]{2,1,0:T(8,128)(2,1)}, u32[]{:S(2)}) copy-start(bf16[1,4096,1024]{2,1,0:T(8,128)(2,1)} %all-gather.3.cloned.1.call-done) | copy-start | bytes 25165828
Sparse Core Ops, SparseCore 0:
  12.1 140.7 all-reduce.1
Sparse Core Ops, SparseCore 1:
  17.7 115.6 reduce-scatter.1
  135.9 73.7 all-gather.2
where the time goes:
time: 231 us; the launch traced here: 227 us
  waiting for transfers between devices  184 us (80%)
  matrix products  17.2 us (7%)
  between operations  15.5 us (7%)
  other arithmetic  10.2 us (4%)
    psum x1, waiting for transfers between devices, body(): summed = lax.psum(pseudo_terms, 'replica')  135 us
    all_gather x1, waiting for transfers between devices, body(): whole = lax.all_gather(weight, 'fsdp', axis=0, tiled=True)  49.2 us
    dot_general x1, matrix products, body(): lax.dot_general(inputs, cotangent, (((0,), (0,)), ((), ())), preferred_el...  6.74 us
    dot_general x1, matrix products, body(): jnp.dot(inputs, whole, preferred_element_type=jnp.float32)  6.65 us
  transfers between devices with their start and end apart: 3, of which 2 were waited for; matrix products, arithmetic and copies ran while one was open for 6% of the time, Pallas kernels for 0%

commit v1 on v0

v1 whole, which is shorter than its diff:
```python
import functools
import jax
import jax.numpy as jnp
import numpy as np
from jax import lax
from jax.experimental import pallas as pl
from jax.experimental.pallas import tpu as pltpu
from jax.sharding import PartitionSpec as P

first_bias = 0.9999734386011124
second_bias = 0.9940794707796655
BF, F32 = jnp.bfloat16, jnp.float32
B = 256
KV = 1024
D = 4096

RELATIVE = ((1, 2), (1, 1), (1, 3), (1, 0), (0, 2), (0, 1), (0, 3), (0, 0))


def places():
    table = np.zeros((256, 24), np.int32)
    for rep in range(16):
        for me in range(16):
            core, x, half = me % 2, me // 2 % 4, me // 8
            row = table[rep * 16 + me]
            for k, (dh, dx) in enumerate(RELATIVE):
                first = (half ^ dh) * 8 + (x + dx) % 4 * 2
                row[k], row[8 + k] = first + core, first + 1 - core
            row[16], row[17], row[18] = rep & 1, rep >> 1 & 1, rep >> 2 & 1
            row[19] = row[16] * 4 + row[17] * 2 + row[18]
    return table


def send(value, dx=0, half=0, core=0):
    pairs = [
        (h * 8 + x * 2 + c, (h ^ half) * 8 + (x + dx) % 4 * 2 + (c ^ core))
        for h in range(2)
        for x in range(4)
        for c in range(2)
    ]
    return lax.ppermute(value, "fsdp", pairs)


def swap(value, bit):
    return lax.ppermute(value, "replica", [(r, r ^ bit) for r in range(16)])


def tdot(a, b):
    return lax.dot_general(a, b, (((0,), (0,)), ((), ())), preferred_element_type=F32)


def ndot(a, b):
    return lax.dot_general(a, b, (((1,), (1,)), ((), ())), preferred_element_type=F32)


def at(shape, row=0, col=0):
    def index(k, s):
        pick = lambda p: p(k, s) if callable(p) else p
        return (pick(row), pick(col))

    return pl.BlockSpec(shape, index)


class Steps:
    def __init__(self, scalars):
        self.scalars = scalars
        self.last = None

    def __call__(self, kernel, ins, outs, grid=1, limit=24, flops=0):
        arrays, specs = [a for a, _ in ins], [s for _, s in ins]
        if self.last is not None:
            arrays.append(self.last)
            specs.append(pl.BlockSpec(memory_space=pl.ANY))
        n, tied = len(ins), self.last is not None

        def run(s, *refs):
            kernel(s, *refs[:n], *refs[n + tied :])

        result = pl.pallas_call(
            run,
            out_shape=[jax.ShapeDtypeStruct(shape, dtype) for shape, dtype, _ in outs],
            grid_spec=pltpu.PrefetchScalarGridSpec(
                num_scalar_prefetch=1,
                grid=(grid,),
                in_specs=specs,
                out_specs=[spec for _, _, spec in outs],
            ),
            compiler_params=pltpu.CompilerParams(vmem_limit_bytes=limit * 2**20),
            cost_estimate=pl.CostEstimate(flops=flops, bytes_accessed=1000, transcendentals=0),
        )(self.scalars, *arrays)
        self.last = result[0]
        return result


def pack_kernel(s, *refs):
    for k in range(8):
        refs[10][:, k * B : (k + 1) * B] = refs[k][...]
    refs[10][:, 2 * KV :] = refs[8][...]
    refs[11][...] = refs[9][...]


def grad_kernel(s, h, ph, c, pc, out):
    out[...] = (tdot(h[...], c[...]) + tdot(ph[...], pc[...])).astype(BF)


def two_kernel(s, h, ph, c, pc, out, last):
    value = (tdot(h[...], c[...]) + tdot(ph[...], pc[...])).astype(BF)

    @pl.when(pl.program_id(0) < 2)
    def _():
        out[...] = value

    @pl.when(pl.program_id(0) == 2)
    def _():
        last[...] = value


def add_kernel(s, h, ph, c, pc, came, out):
    out[...] = (tdot(h[...], c[...]) + tdot(ph[...], pc[...]) + came[...].astype(F32)).astype(BF)


def add_two_kernel(s, h, ph, c, pc, came, one, two):
    value = (tdot(h[...], c[...]) + tdot(ph[...], pc[...]) + came[...].astype(F32)).astype(BF)

    @pl.when(pl.program_id(0) == 0)
    def _():
        one[...] = value

    @pl.when(pl.program_id(0) == 1)
    def _():
        two[...] = value


def adam_kernel(s, h, ph, c, pc, r0, r1, r2, r3, w, m, v, nw, nm, nv):
    grad = tdot(h[...], c[...]) + tdot(ph[...], pc[...])
    grad = grad + r0[...].astype(F32)
    grad = grad + r1[...].astype(F32)
    grad = grad + r2[...].astype(F32)
    grad = grad + r3[...].astype(F32)
    first = 0.9 * m[...] + 0.1 * grad
    second = 0.95 * v[...] + 0.05 * grad * grad
    nm[...] = first
    nv[...] = second
    update = first / first_bias / (jnp.sqrt(second / second_bias) + 1e-08)
    old = w[...].astype(F32)
    nw[...] = (old - 0.003 * (update + 0.1 * old)).astype(BF)


def forward_kernel(s, wh, wl, wr, left, right):
    left[:B] = wh[...]
    left[B:] = wl[...]
    right[:B] = wh[...]
    right[B:] = wr[...]


def copy_two_kernel(s, a, b, left, right):
    left[...] = a[...]
    right[...] = b[...]


def use(hs, phs, c, pc, ws, gi, put):
    a = p = None
    for i, w in enumerate(ws):
        ta = jnp.dot(hs[i][...], w, preferred_element_type=F32)
        tp = jnp.dot(phs[i][...], w, preferred_element_type=F32)
        a, p = (ta, tp) if a is None else (a + ta, p + tp)
        cols = slice(i * B, (i + 1) * B)
        gi[:, cols] = ndot(c[...], w).astype(BF)
        put(cols, ndot(pc[...], w).astype(BF))
    return a, p


def near_kernel(s, *refs):
    hs, phs, (c, pc), ws = refs[:4], refs[4:8], refs[8:10], refs[10:14]
    a, p, gi, pgi = refs[14:]

    def put(cols, value):
        pgi[:, cols] = value

    a[...], p[...] = use(hs, phs, c, pc, [w[...] for w in ws], gi, put)


def far_kernel(s, *refs):
    hs, phs, (c, pc), (l, r, ll, rr) = refs[:4], refs[4:8], refs[8:10], refs[10:14]
    a0, p0, pgi0 = refs[14:17]
    a, gi, out = refs[17:]

    def put(cols, value):
        out[:, slice(KV + cols.start, KV + cols.stop)] = value

    ws = [
        l[:B],
        r[:B],
        jnp.concatenate([l[B:], r[B:]], axis=0),
        jnp.concatenate([ll[...], rr[...]], axis=0),
    ]
    own, peer = use(hs, phs, c, pc, ws, gi, put)
    a[...] = a0[...] + own
    out[:, :KV] = pgi0[...]
    peer = p0[...] + peer
    high = peer.astype(BF)
    out[:, 2 * KV : 3 * KV] = high
    out[:, 3 * KV :] = (peer - high.astype(F32)).astype(BF)


NEAR, FAR = (7, 3, 6, 5), (2, 1, 4, 0)


def finish_kernel(s, a, gi0, gi1, came, keys, out):
    high = came[:, 2 * KV : 3 * KV].astype(F32)
    low = came[:, 3 * KV :].astype(F32)
    keys[...] = (a[...] + (high + low)).astype(BF)
    for j, (order, own) in enumerate(((NEAR, gi0), (FAR, gi1))):
        for i, k in enumerate(order):
            cols = slice(i * B, (i + 1) * B)
            out[:, pl.ds(pl.multiple_of(s[k] * B, B), B)] = own[:, cols]
            other = slice(j * KV + i * B, j * KV + (i + 1) * B)
            out[:, pl.ds(pl.multiple_of(s[8 + k] * B, B), B)] = came[:, other]


def sum1_kernel(s, local, came, keep, give):
    total = local[...].astype(F32) + came[...].astype(F32)
    low, high = total[:64], total[64:]
    mine = s[17] == 0
    keep[...] = jnp.where(mine, low, high)
    give[...] = jnp.where(mine, high, low)


def sum2_kernel(s, held, came, keep, give):
    total = held[...] + came[...]
    low, high = total[:32], total[32:]
    mine = s[18] == 0
    keep[...] = jnp.where(mine, low, high)
    give[...] = jnp.where(mine, high, low)


def sum3_kernel(s, held, came, out):
    out[...] = held[...] + came[...]


def pseudo_kernel(s, held, came, whole, out):
    out[...] = (whole[...] - (held[...] + came[...]) / 16).astype(BF)


def join(first, a, b):
    return jnp.concatenate([jnp.where(first, a, b), jnp.where(first, b, a)], axis=0)


def join_kernel(slot, s, a, b, out):
    out[...] = join(s[slot] == 0, a[...].astype(F32), b[...].astype(F32)).astype(BF)


def merge_kernel(s, a, b, whole, momentum, new_global, new_momentum):
    pseudo = join(s[16] == 0, a[...].astype(F32), b[...].astype(F32))
    after = 0.9 * momentum[...] + pseudo
    new_momentum[...] = after
    new_global[...] = whole[...] - 0.7 * (pseudo + 0.9 * after)


def body(hidden, key_weight, adam_first, adam_second, key_cotangent, frag_global, frag_momentum, frag_local):
    h, w, c = hidden[0], key_weight[0], key_cotangent[0]
    local = frag_local[0]
    device = lax.axis_index("replica") * 16 + lax.axis_index("fsdp")
    step = Steps(lax.dynamic_index_in_dim(jnp.asarray(places()), device, keepdims=False))
    full, square = (B, KV), (B, B)

    def own(k):
        return (h, at(square, 0, lambda _, s, k=k: s[k]))

    def rows(n, row=0):
        return at((n, KV), row)

    w_half = send(w, half=1)
    w_left = send(w, dx=1)
    w_right = send(w, dx=3)

    packed, give = step(
        pack_kernel,
        [(h, at(square, 0, lambda _, s, k=k: s[8 + k])) for k in range(8)]
        + [(c, at(full)), (local, rows(128, lambda _, s: 1 - s[16]))],
        [((B, 3 * KV), BF, at((B, 3 * KV))), ((128, KV), BF, rows(128))],
    )
    peer = send(packed, core=1)
    f1 = swap(give, 1)

    def operands(base):
        return [
            (h, at(square, 0, lambda k, s: s[base + k])),
            (peer, at(square, 0, lambda k, s: base + k)),
            (c, at(full)),
            (peer, at(full, 0, 2)),
        ]

    keep, give = step(
        sum1_kernel,
        [(local, rows(128, lambda _, s: s[16])), (f1, rows(128))],
        [((64, KV), F32, rows(64))] * 2,
    )
    f2 = swap(give, 2)

    (out0,) = step(grad_kernel, operands(0), [(full, BF, at(full))])
    y0 = send(out0, half=1)
    out1, out2 = step(
        two_kernel,
        operands(1),
        [((2 * B, KV), BF, at(full, lambda k, s: jnp.minimum(k, 1))), (full, BF, at(full))],
        grid=3,
    )

    left, right = step(
        forward_kernel,
        [(w_half, at(full)), (w_left, rows(128)), (w_right, rows(128, 1))],
        [((384, KV), BF, rows(384))] * 2,
    )
    s2l = send(left, dx=1)
    s2r = send(right, dx=3)
    y1 = send(out1, half=1)

    acc_a, acc_p, gi0, pgi0 = step(
        near_kernel,
        [own(k) for k in NEAR]
        + [(peer, at(square, 0, k)) for k in NEAR]
        + [(c, at(full)), (peer, at(full, 0, 2))]
        + [(a, at(full)) for a in (w, w_half, w_left, w_right)],
        [(full, F32, at(full))] * 2 + [(full, BF, at(full))] * 2,
    )
    keep, give = step(
        sum2_kernel, [(keep, rows(64)), (f2, rows(64))], [((32, KV), F32, rows(32))] * 2
    )
    f3 = swap(give, 4)

    (sum0,) = step(add_kernel, operands(4) + [(y0, at(full))], [(full, BF, at(full))])
    x2 = send(sum0, dx=2)

    (total,) = step(sum3_kernel, [(keep, rows(32)), (f3, rows(32))], [((32, KV), F32, rows(32))])
    f4 = swap(total, 8)

    left, right = step(
        copy_two_kernel, [(s2l, rows(128)), (s2r, rows(128, 1))], [((128, KV), BF, rows(128))] * 2
    )
    s3l = send(left, dx=1)
    s3r = send(right, dx=3)
    y2 = send(out2, half=1)

    (pseudo,) = step(
        pseudo_kernel,
        [(total, rows(32)), (f4, rows(32)), (frag_global, rows(32, lambda _, s: s[19]))],
        [((32, KV), BF, rows(32))],
    )
    f5 = swap(pseudo, 4)

    acc, gi1, back = step(
        far_kernel,
        [own(k) for k in FAR]
        + [(peer, at(square, 0, k)) for k in FAR]
        + [(c, at(full)), (peer, at(full, 0, 2))]
        + [(s2l, rows(384)), (s2r, rows(384)), (s3l, rows(128)), (s3r, rows(128))]
        + [(a, at(full)) for a in (acc_a, acc_p, pgi0)],
        [(full, F32, at(full)), (full, BF, at(full)), ((B, D), BF, at((B, D)))],
        limit=40,
    )
    got = send(back, core=1)

    (pseudo,) = step(
        functools.partial(join_kernel, 18),
        [(pseudo, rows(32)), (f5, rows(32))],
        [((64, KV), BF, rows(64))],
    )
    f6 = swap(pseudo, 2)

    sum1, sum3 = step(
        add_two_kernel,
        operands(5) + [(y1, at(full, lambda k, s: k))],
        [(full, BF, at(full))] * 2,
        grid=2,
    )
    x1 = send(sum1, dx=1)
    x3 = send(sum3, dx=3)

    (pseudo,) = step(
        functools.partial(join_kernel, 17),
        [(pseudo, rows(64)), (f6, rows(64))],
        [((128, KV), BF, rows(128))],
    )
    f7 = swap(pseudo, 1)

    keys, input_grad = step(
        finish_kernel,
        [(acc, at(full)), (gi0, at(full)), (gi1, at(full)), (got, at((B, D)))],
        [(full, BF, at(full)), ((B, D), BF, at((B, D)))],
    )
    tile = at((B, B), 0, lambda k, s: k)
    new_global, new_momentum = step(
        merge_kernel,
        [(pseudo, at((128, B), 0, lambda k, s: k)), (f7, at((128, B), 0, lambda k, s: k))]
        + [(frag_global, tile), (frag_momentum, tile)],
        [(full, F32, tile)] * 2,
        grid=4,
    )
    new_weight, new_first, new_second = step(
        adam_kernel,
        [own(7), (peer, at(square, 0, 7)), (c, tile), (peer, at(square, 0, lambda k, s: 8 + k))]
        + [(a, tile) for a in (y2, x2, x1, x3, w, adam_first[0], adam_second[0])],
        [(full, BF, tile), (full, F32, tile), (full, F32, tile)],
        grid=4,
    )
    return (
        keys[None],
        input_grad[None],
        new_weight[None],
        new_first[None],
        new_second[None],
        new_global,
        new_momentum,
    )


def solution(mesh):
    rows = P("replica", "fsdp", None)
    return jax.shard_map(
        body,
        mesh=mesh,
        in_specs=(rows,) * 5 + (P("fsdp", None),) * 2 + (rows,),
        out_specs=(rows,) * 5 + (P("fsdp", None),) * 2,
        check_vma=False,
    )
```

time: 231 us -> 119 us (0.52); the launches traced: 227 us -> 119 us
  waiting for transfers between devices: 184 us -> 52.7 us
  starting transfers between devices: 0.13 us -> 31.3 us
  Pallas kernels: 0 us -> 26.9 us
  matrix products: 17.2 us -> 0 us
  between operations: 15.5 us -> 0.91 us
  other arithmetic: 10.2 us -> 0 us
  local copies, waits for them, and re-layouts: 0.02 us -> 6.84 us
    psum x1 -> x0, waiting for transfers between devices: 135 us -> none  [body(): summed = lax.psum(pseudo_terms, 'replica')]
    ppermute x0 -> x22, waiting for transfers between devices: none -> 52.7 us  [the longest x7 33.7 us: swap(): return lax.ppermute(value, 'replica', [(r, r ^ bit) for r in range(16)])]
    all_gather x1 -> x0, waiting for transfers between devices: 49.2 us -> none  [body(): whole = lax.all_gather(weight, 'fsdp', axis=0, tiled=True)]
    ppermute x0 -> x22, starting transfers between devices: none -> 31.3 us  [the longest x15 17.5 us: send(): return lax.ppermute(value, 'fsdp', pairs)]
    pallas_call x0 -> x18, Pallas kernels: none -> 26.9 us  [__call__(): pl.pallas_call(run, out_shape=[jax.ShapeDtypeStruct(shape, dtype) for sha...]
    dot_general x3 -> x0, matrix products: 17.2 us -> none  [the longest x1 6.74 us: body(): lax.dot_general(inputs, cotangent, (((0,), (0,)), ((), ())), preferred_el...]
    unnamed x8 -> x26, local copies, waits for them, and re-layouts: 0.02 us -> 6.14 us
    sub x2 -> x0, other arithmetic: 5.97 us -> none  [the longest x1 3.32 us: body(): new_global = frag_global - 0.7 * (pseudo + 0.9 * new_momentum)]
  transfers between devices with their start and end apart: 3 -> 22, of which waited for: 2 -> 10; matrix products, arithmetic and copies ran while one was open for 6% -> 0% of each run, Pallas kernels for 0% -> 15%
where the time goes in v1:
time: 119 us
  waiting for transfers between devices  52.7 us (44%)
  starting transfers between devices  31.3 us (26%)
  Pallas kernels  26.9 us (23%)
  local copies, waits for them, and re-layouts  6.84 us (6%)
    ppermute x7, waiting for transfers between devices, swap(): return lax.ppermute(value, 'replica', [(r, r ^ bit) for r in range(16)])  33.7 us
    pallas_call x18, Pallas kernels, __call__(): pl.pallas_call(run, out_shape=[jax.ShapeDtypeStruct(shape, dtype) for sha...  26.9 us
    ppermute x15, waiting for transfers between devices, send(): return lax.ppermute(value, 'fsdp', pairs)  19 us
    ppermute x15, starting transfers between devices, send(): return lax.ppermute(value, 'fsdp', pairs)  17.5 us
    ppermute x7, starting transfers between devices, swap(): return lax.ppermute(value, 'replica', [(r, r ^ bit) for r in range(16)])  13.7 us
    unnamed x26, local copies, waits for them, and re-layouts  6.14 us
  transfers between devices with their start and end apart: 22, of which 10 were waited for; matrix products, arithmetic and copies ran while one was open for 0% of the time, Pallas kernels for 15%

profile of v1, /device:TPU:6, one launch (start us, length us, event | category | flops | bytes accessed | tf_op | source)
XLA Modules:
  0.0 118.7 jit_solution(14124139775898962309)
XLA Ops:
  6.1 3.2 %collective-permute-start.1 = (bf16[256,1024]{1,0:T(8,128)(2,1)S(1)}, bf16[256,1024]{1,0:T(8,128)(2,1)S(1)}, u32[]{:S(2)}, u32[]{:S(2)}) collective-permute-start(bf16[256,1024]{1,0:T(8,128)(2,1)S(1)} %bitcast.44), channel_id=1, source_target_pairs={{0,8},{1,9},{2,10},{3,11},{4,12},{5,13},{6,14},{7,15},{8,0},{9,1},... | collective-permute-start | bytes 1572872 | tf_op jit(solution)/shard_map/ppermute | solution.py:41
  11.3 1.9 %collective-permute-start.4 = (bf16[128,1024]{1,0:T(8,128)(2,1)S(1)}, bf16[128,1024]{1,0:T(8,128)(2,1)S(1)}, u32[]{:S(2)}, u32[]{:S(2)}) collective-permute-start(bf16[128,1024]{1,0:T(8,128)(2,1)S(1)} %get-tuple-element.36), channel_id=1, source_target_pairs={{0,16},{16,0},{32,48},{48,32},{64,80},{80,64},{96,112},{112,96},{1... | collective-permute-start | bytes 786440 | tf_op jit(solution)/shard_map/ppermute | solution.py:45
  13.2 6.0 %collective-permute-done.4.refs_1_ = bf16[128,1024]{1,0:T(8,128)(2,1)S(1)} collective-permute-done((bf16[128,1024]{1,0:T(8,128)(2,1)S(1)}, bf16[128,1024]{1,0:T(8,128)(2,1)S(1)}, u32[]{:S(2)}, u32[]{:S(2)}) %collective-permute-start.4) | collective-permute-done | bytes 262176 | tf_op jit(solution)/shard_map/ppermute | solution.py:45
  20.8 2.3 %shard_map.147 = (bf16[512,1024]{1,0:T(8,128)(2,1)S(1)}, bf16[256,1024]{1,0:T(8,128)(2,1)S(1)}) custom-call(s32[24]{0:T(128)S(1)} %dynamic-slice_bitcast_fusion.s, bf16[256,4096]{1,0:T(8,128)(2,1)S(1)} %bitcast.22, bf16[256,3072]{1,0:T(8,128)(2,1)S(1)} %collective-permute-done.refs_1_.refs_3_.refs_4_.refs_5_.refs_6_.refs_7_.refs_9_, ...), custom_call_target="tpu_custom_call" | custom-call | bytes 1000 | tf_op jit(solution)/shard_map/pallas_call | solution.py:79
  25.6 1.7 %collective-permute-start.6 = (bf16[384,1024]{1,0:T(8,128)(2,1)S(1)}, bf16[384,1024]{1,0:T(8,128)(2,1)S(1)}, u32[]{:S(2)}, u32[]{:S(2)}) collective-permute-start(bf16[384,1024]{1,0:T(8,128)(2,1)S(1)} %get-tuple-element.40), channel_id=1, source_target_pairs={{0,6},{1,7},{2,0},{3,1},{4,2},{5,3},{6,4},{7,5},{8,14},{9,15},{10,... | collective-permute-start | bytes 2359304 | tf_op jit(solution)/shard_map/ppermute | solution.py:41
  27.3 2.1 %collective-permute-start.9 = (bf16[256,1024]{1,0:T(8,128)(2,1)S(1)}, bf16[256,1024]{1,0:T(8,128)(2,1)S(1)}, u32[]{:S(2)}, u32[]{:S(2)}) collective-permute-start(bf16[256,1024]{1,0:T(8,128)(2,1)S(1)} %shard_map.146.refs_4_), channel_id=1, source_target_pairs={{0,8},{1,9},{2,10},{3,11},{4,12},{5,13},{6,14},{7,15},{8,0},{9,1},... | collective-permute-start | bytes 1572872 | tf_op jit(solution)/shard_map/ppermute | solution.py:41
  30.9 3.0 %shard_map.149 = (f32[256,1024]{1,0:T(8,128)S(1)}, f32[256,1024]{1,0:T(8,128)S(1)}, bf16[256,1024]{1,0:T(8,128)(2,1)S(1)}, bf16[256,1024]{1,0:T(8,128)(2,1)S(1)}) custom-call(s32[24]{0:T(128)S(1)} %dynamic-slice_bitcast_fusion.s, bf16[256,4096]{1,0:T(8,128)(2,1)S(1)} %bitcast.23, bf16[256,4096]{1,0:T(8,128)(2,1)S(1)} %bitcast.24, ...), custom_call_target="tpu_custom_call" | custom-call | bytes 1000 | tf_op jit(solution)/shard_map/pallas_call | solution.py:79
  33.9 8.2 %collective-permute-done.7.refs_1_ = f32[64,1024]{1,0:T(8,128)S(1)} collective-permute-done((f32[64,1024]{1,0:T(8,128)S(1)}, f32[64,1024]{1,0:T(8,128)S(1)}, u32[]{:S(2)}, u32[]{:S(2)}) %collective-permute-start.7) | collective-permute-done | bytes 262176 | tf_op jit(solution)/shard_map/ppermute | solution.py:45
  42.7 6.3 %collective-permute-start.8 = (f32[32,1024]{1,0:T(8,128)S(1)}, f32[32,1024]{1,0:T(8,128)S(1)}, u32[]{:S(2)}, u32[]{:S(2)}) collective-permute-start(f32[32,1024]{1,0:T(8,128)S(1)} %get-tuple-element.44), channel_id=1, source_target_pairs={{0,64},{16,80},{32,96},{48,112},{64,0},{80,16},{96,32},{112,48},{1... | collective-permute-start | bytes 393224 | tf_op jit(solution)/shard_map/ppermute | solution.py:45
  50.0 4.9 %collective-permute-done.8.refs_1_ = f32[32,1024]{1,0:T(8,128)S(1)} collective-permute-done((f32[32,1024]{1,0:T(8,128)S(1)}, f32[32,1024]{1,0:T(8,128)S(1)}, u32[]{:S(2)}, u32[]{:S(2)}) %collective-permute-start.8) | collective-permute-done | bytes 131104 | tf_op jit(solution)/shard_map/ppermute | solution.py:45
  56.1 1.7 %collective-permute-start.10 = (bf16[128,1024]{1,0:T(8,128)(2,1)S(1)}, bf16[128,1024]{1,0:T(8,128)(2,1)S(1)}, u32[]{:S(2)}, u32[]{:S(2)}) collective-permute-start(bf16[128,1024]{1,0:T(8,128)(2,1)S(1)} %get-tuple-element.45.refs_3_), channel_id=1, source_target_pairs={{0,2},{1,3},{2,4},{3,5},{4,6},{5,7},{6,0},{7,1},{8,10},{9,11},{10,... | collective-permute-start | bytes 786440 | tf_op jit(solution)/shard_map/ppermute | solution.py:41
  59.0 4.1 %collective-permute-done.12.refs_1_ = f32[32,1024]{1,0:T(8,128)S(1)} collective-permute-done((f32[32,1024]{1,0:T(8,128)S(1)}, f32[32,1024]{1,0:T(8,128)S(1)}, u32[]{:S(2)}, u32[]{:S(2)}) %collective-permute-start.12) | collective-permute-done | bytes 131104 | tf_op jit(solution)/shard_map/ppermute | solution.py:45
  63.7 1.6 %collective-permute-done.11.refs_13_ = bf16[128,1024]{1,0:T(8,128)(2,1)S(1)} collective-permute-done((bf16[128,1024]{1,0:T(8,128)(2,1)S(1)}, bf16[128,1024]{1,0:T(8,128)(2,1)S(1)}, u32[]{:S(2)}, u32[]{:S(2)}) %collective-permute-start.11) | collective-permute-done | bytes 262176 | tf_op jit(solution)/shard_map/ppermute | solution.py:41
  65.4 3.0 %shard_map.155 = (f32[256,1024]{1,0:T(8,128)S(1)}, bf16[256,1024]{1,0:T(8,128)(2,1)S(1)}, bf16[256,4096]{1,0:T(8,128)(2,1)S(1)}) custom-call(s32[24]{0:T(128)S(1)} %dynamic-slice_bitcast_fusion.s, bf16[256,4096]{1,0:T(8,128)(2,1)S(1)} %bitcast.28, bf16[256,4096]{1,0:T(8,128)(2,1)S(1)} %bitcast.29, bf16[256,4096]{1,0:T(8,128)(2,1)S(1)} %bitcast.30, ...), custom_call_target="tpu_custom_call" | custom-call | bytes 1000 | tf_op jit(solution)/shard_map/pallas_call | solution.py:79
  68.5 2.7 %collective-permute-start.16 = (bf16[512,1024]{1,0:T(8,128)(2,1)S(1)}, bf16[512,1024]{1,0:T(8,128)(2,1)S(1)}, u32[]{:S(2)}, u32[]{:S(2)}) collective-permute-start(bf16[512,1024]{1,0:T(8,128)(2,1)S(1)} %get-tuple-element.38.refs_3_), channel_id=1, source_target_pairs={{0,8},{1,9},{2,10},{3,11},{4,12},{5,13},{6,14},{7,15},{8,0},{9,1},... | collective-permute-start | bytes 3145736 | tf_op jit(solution)/shard_map/ppermute | solution.py:41
  71.2 2.9 %collective-permute-start.14 = (bf16[32,1024]{1,0:T(8,128)(2,1)S(1)}, bf16[32,1024]{1,0:T(8,128)(2,1)S(1)}, u32[]{:S(2)}, u32[]{:S(2)}) collective-permute-start(bf16[32,1024]{1,0:T(8,128)(2,1)S(1)} %shard_map.154.refs_17_.refs_0_), channel_id=1, source_target_pairs={{0,64},{16,80},{32,96},{48,112},{64,0},{80,16},{96,32},{112,48},{1... | collective-permute-start | bytes 196616 | tf_op jit(solution)/shard_map/ppermute | solution.py:45
  74.2 6.1 %collective-permute-done.14.refs_1_ = bf16[32,1024]{1,0:T(8,128)(2,1)S(1)} collective-permute-done((bf16[32,1024]{1,0:T(8,128)(2,1)S(1)}, bf16[32,1024]{1,0:T(8,128)(2,1)S(1)}, u32[]{:S(2)}, u32[]{:S(2)}) %collective-permute-start.14) | collective-permute-done | bytes 65568 | tf_op jit(solution)/shard_map/ppermute | solution.py:45
  81.9 14.1 %collective-permute-done.16.refs_4_ = bf16[512,1024]{1,0:T(8,128)(2,1)S(1)} collective-permute-done((bf16[512,1024]{1,0:T(8,128)(2,1)S(1)}, bf16[512,1024]{1,0:T(8,128)(2,1)S(1)}, u32[]{:S(2)}, u32[]{:S(2)}) %collective-permute-start.16) | collective-permute-done | bytes 1048608 | tf_op jit(solution)/shard_map/ppermute | solution.py:41
  96.1 1.7 %shard_map.157 = (bf16[256,1024]{1,0:T(8,128)(2,1)S(1)}, bf16[256,1024]{1,0:T(8,128)(2,1)S(1)}) custom-call(s32[24]{0:T(128)S(1)} %dynamic-slice_bitcast_fusion.s, bf16[256,4096]{1,0:T(8,128)(2,1)S(1)} %bitcast.32, bf16[256,3072]{1,0:T(8,128)(2,1)S(1)} %collective-permute-done.refs_1_.refs_3_.refs_4_.refs_5_.refs_6_.refs_7_.refs_9_, ...), custom_call_target="tpu_custom_call" | custom-call | bytes 1000 | tf_op jit(solution)/shard_map/pallas_call | solution.py:79
  100.7 2.4 %shard_map.159 = (bf16[256,1024]{1,0:T(8,128)(2,1)}, bf16[256,4096]{1,0:T(8,128)(2,1)}) custom-call(s32[24]{0:T(128)S(1)} %dynamic-slice_bitcast_fusion.s, f32[256,1024]{1,0:T(8,128)S(1)} %get-tuple-element.49.refs_2_.refs_0_, bf16[256,1024]{1,0:T(8,128)(2,1)S(1)} %get-tuple-element.50.refs_1_, bf16[256,1024]{1,0:T(8,128)(2,1)S(1)} %get-tuple-element.51.refs_2_, ...), custom_call_target="tpu_custom_call" | custom-call | bytes 1000 | tf_op jit(solution)/shard_map/pallas_call | solution.py:79
  103.1 4.4 %collective-permute-done.21.refs_1_ = bf16[128,1024]{1,0:T(8,128)(2,1)S(1)} collective-permute-done((bf16[128,1024]{1,0:T(8,128)(2,1)S(1)}, bf16[128,1024]{1,0:T(8,128)(2,1)S(1)}, u32[]{:S(2)}, u32[]{:S(2)}) %collective-permute-start.21) | collective-permute-done | bytes 262176 | tf_op jit(solution)/shard_map/ppermute | solution.py:45
  108.5 2.6 %shard_map.160 = (f32[256,1024]{1,0:T(8,128)}, f32[256,1024]{1,0:T(8,128)}) custom-call(s32[24]{0:T(128)S(1)} %dynamic-slice_bitcast_fusion.s, bf16[128,1024]{1,0:T(8,128)(2,1)S(1)} %shard_map.158.refs_4_.refs_0_, bf16[128,1024]{1,0:T(8,128)(2,1)S(1)} %collective-permute-done.21.refs_1_, f32[256,1024]{1,0:T(8,128)S(1)} %copy-done.4, ...), custom_call_target="tpu_custom_call" | custom-call | bytes 1000 | tf_op jit(solution)/shard_map/pallas_call | solution.py:79
  111.2 1.9 %collective-permute-done.20.refs_7_ = bf16[256,1024]{1,0:T(8,128)(2,1)S(1)} collective-permute-done((bf16[256,1024]{1,0:T(8,128)(2,1)S(1)}, bf16[256,1024]{1,0:T(8,128)(2,1)S(1)}, u32[]{:S(2)}, u32[]{:S(2)}) %collective-permute-start.20) | collective-permute-done | bytes 524320 | tf_op jit(solution)/shard_map/ppermute | solution.py:41
  114.3 4.4 %shard_map.161 = (bf16[256,1024]{1,0:T(8,128)(2,1)}, f32[256,1024]{1,0:T(8,128)}, f32[256,1024]{1,0:T(8,128)}) custom-call(s32[24]{0:T(128)S(1)} %dynamic-slice_bitcast_fusion.s, bf16[256,4096]{1,0:T(8,128)(2,1)S(1)} %bitcast.33, bf16[256,3072]{1,0:T(8,128)(2,1)S(1)} %collective-permute-done.refs_1_.refs_3_.refs_4_.refs_5_.refs_6_.refs_7_.refs_9_, ...), custom_call_target="tpu_custom_call" | custom-call | bytes 1000 | tf_op jit(solution)/shard_map/pallas_call | solution.py:79
  (65 shorter events, 24.4 us)
Async XLA Ops:
  5.0 14.1 %copy-start.6 = (bf16[1,256,1024]{2,1,0:T(8,128)(2,1)S(1)}, bf16[1,256,1024]{2,1,0:T(8,128)(2,1)}, u32[]{:S(2)}) copy-start(bf16[1,256,1024]{2,1,0:T(8,128)(2,1)} %param.16) | copy-start | bytes 1572868
  5.0 14.8 %copy-start.3 = (bf16[1,256,1024]{2,1,0:T(8,128)(2,1)S(1)}, bf16[1,256,1024]{2,1,0:T(8,128)(2,1)}, u32[]{:S(2)}) copy-start(bf16[1,256,1024]{2,1,0:T(8,128)(2,1)} %param.13) | copy-start | bytes 1572868
  5.8 14.0 %collective-permute-start = (bf16[256,3072]{1,0:T(8,128)(2,1)S(1)}, bf16[256,3072]{1,0:T(8,128)(2,1)S(1)}, u32[]{:S(2)}, u32[]{:S(2)}) collective-permute-start(bf16[256,3072]{1,0:T(8,128)(2,1)S(1)} %get-tuple-element.35.refs_2_), channel_id=1, source_target_pairs={{0,1},{1,0},{2,3},{3,2},{4,5},{5,4},{6,7},{7,6},{8,9},{9,8},{10,11... | collective-permute-start | bytes 4718600 | tf_op jit(solution)/shard_map/ppermute | solution.py:41
  6.1 17.1 %collective-permute-start.1 = (bf16[256,1024]{1,0:T(8,128)(2,1)S(1)}, bf16[256,1024]{1,0:T(8,128)(2,1)S(1)}, u32[]{:S(2)}, u32[]{:S(2)}) collective-permute-start(bf16[256,1024]{1,0:T(8,128)(2,1)S(1)} %bitcast.44), channel_id=1, source_target_pairs={{0,8},{1,9},{2,10},{3,11},{4,12},{5,13},{6,14},{7,15},{8,0},{9,1},... | collective-permute-start | bytes 1572872 | tf_op jit(solution)/shard_map/ppermute | solution.py:41
  9.2 13.9 %collective-permute-start.2 = (bf16[256,1024]{1,0:T(8,128)(2,1)S(1)}, bf16[256,1024]{1,0:T(8,128)(2,1)S(1)}, u32[]{:S(2)}, u32[]{:S(2)}) collective-permute-start(bf16[256,1024]{1,0:T(8,128)(2,1)S(1)} %bitcast.45), channel_id=1, source_target_pairs={{0,2},{1,3},{2,4},{3,5},{4,6},{5,7},{6,0},{7,1},{8,10},{9,11},{10,... | collective-permute-start | bytes 1572872 | tf_op jit(solution)/shard_map/ppermute | solution.py:41
  9.7 14.8 %collective-permute-start.3 = (bf16[256,1024]{1,0:T(8,128)(2,1)S(1)}, bf16[256,1024]{1,0:T(8,128)(2,1)S(1)}, u32[]{:S(2)}, u32[]{:S(2)}) collective-permute-start(bf16[256,1024]{1,0:T(8,128)(2,1)S(1)} %bitcast.46), channel_id=1, source_target_pairs={{0,6},{1,7},{2,0},{3,1},{4,2},{5,3},{6,4},{7,5},{8,14},{9,15},{10,... | collective-permute-start | bytes 1572872 | tf_op jit(solution)/shard_map/ppermute | solution.py:41
  11.3 7.9 %collective-permute-start.4 = (bf16[128,1024]{1,0:T(8,128)(2,1)S(1)}, bf16[128,1024]{1,0:T(8,128)(2,1)S(1)}, u32[]{:S(2)}, u32[]{:S(2)}) collective-permute-start(bf16[128,1024]{1,0:T(8,128)(2,1)S(1)} %get-tuple-element.36), channel_id=1, source_target_pairs={{0,16},{16,0},{32,48},{48,32},{64,80},{80,64},{96,112},{112,96},{1... | collective-permute-start | bytes 786440 | tf_op jit(solution)/shard_map/ppermute | solution.py:45
  25.2 30.3 %collective-permute-start.5 = (bf16[384,1024]{1,0:T(8,128)(2,1)S(1)}, bf16[384,1024]{1,0:T(8,128)(2,1)S(1)}, u32[]{:S(2)}, u32[]{:S(2)}) collective-permute-start(bf16[384,1024]{1,0:T(8,128)(2,1)S(1)} %get-tuple-element.39.refs_14_), channel_id=1, source_target_pairs={{0,2},{1,3},{2,4},{3,5},{4,6},{5,7},{6,0},{7,1},{8,10},{9,11},{10,... | collective-permute-start | bytes 2359304 | tf_op jit(solution)/shard_map/ppermute | solution.py:41
  25.6 29.9 %collective-permute-start.6 = (bf16[384,1024]{1,0:T(8,128)(2,1)S(1)}, bf16[384,1024]{1,0:T(8,128)(2,1)S(1)}, u32[]{:S(2)}, u32[]{:S(2)}) collective-permute-start(bf16[384,1024]{1,0:T(8,128)(2,1)S(1)} %get-tuple-element.40), channel_id=1, source_target_pairs={{0,6},{1,7},{2,0},{3,1},{4,2},{5,3},{6,4},{7,5},{8,14},{9,15},{10,... | collective-permute-start | bytes 2359304 | tf_op jit(solution)/shard_map/ppermute | solution.py:41
  27.3 21.7 %collective-permute-start.9 = (bf16[256,1024]{1,0:T(8,128)(2,1)S(1)}, bf16[256,1024]{1,0:T(8,128)(2,1)S(1)}, u32[]{:S(2)}, u32[]{:S(2)}) collective-permute-start(bf16[256,1024]{1,0:T(8,128)(2,1)S(1)} %shard_map.146.refs_4_), channel_id=1, source_target_pairs={{0,8},{1,9},{2,10},{3,11},{4,12},{5,13},{6,14},{7,15},{8,0},{9,1},... | collective-permute-start | bytes 1572872 | tf_op jit(solution)/shard_map/ppermute | solution.py:41
  29.3 12.8 %collective-permute-start.7 = (f32[64,1024]{1,0:T(8,128)S(1)}, f32[64,1024]{1,0:T(8,128)S(1)}, u32[]{:S(2)}, u32[]{:S(2)}) collective-permute-start(f32[64,1024]{1,0:T(8,128)S(1)} %get-tuple-element.41), channel_id=1, source_target_pairs={{0,32},{16,48},{32,0},{48,16},{64,96},{80,112},{96,64},{112,80},{1... | collective-permute-start | bytes 786440 | tf_op jit(solution)/shard_map/ppermute | solution.py:45
  42.7 12.2 %collective-permute-start.8 = (f32[32,1024]{1,0:T(8,128)S(1)}, f32[32,1024]{1,0:T(8,128)S(1)}, u32[]{:S(2)}, u32[]{:S(2)}) collective-permute-start(f32[32,1024]{1,0:T(8,128)S(1)} %get-tuple-element.44), channel_id=1, source_target_pairs={{0,64},{16,80},{32,96},{48,112},{64,0},{80,16},{96,32},{112,48},{1... | collective-permute-start | bytes 393224 | tf_op jit(solution)/shard_map/ppermute | solution.py:45
  56.1 7.6 %collective-permute-start.10 = (bf16[128,1024]{1,0:T(8,128)(2,1)S(1)}, bf16[128,1024]{1,0:T(8,128)(2,1)S(1)}, u32[]{:S(2)}, u32[]{:S(2)}) collective-permute-start(bf16[128,1024]{1,0:T(8,128)(2,1)S(1)} %get-tuple-element.45.refs_3_), channel_id=1, source_target_pairs={{0,2},{1,3},{2,4},{3,5},{4,6},{5,7},{6,0},{7,1},{8,10},{9,11},{10,... | collective-permute-start | bytes 786440 | tf_op jit(solution)/shard_map/ppermute | solution.py:41
  57.8 7.6 %collective-permute-start.11 = (bf16[128,1024]{1,0:T(8,128)(2,1)S(1)}, bf16[128,1024]{1,0:T(8,128)(2,1)S(1)}, u32[]{:S(2)}, u32[]{:S(2)}) collective-permute-start(bf16[128,1024]{1,0:T(8,128)(2,1)S(1)} %get-tuple-element.46), channel_id=1, source_target_pairs={{0,6},{1,7},{2,0},{3,1},{4,2},{5,3},{6,4},{7,5},{8,14},{9,15},{10,... | collective-permute-start | bytes 786440 | tf_op jit(solution)/shard_map/ppermute | solution.py:41
  58.2 5.0 %collective-permute-start.12 = (f32[32,1024]{1,0:T(8,128)S(1)}, f32[32,1024]{1,0:T(8,128)S(1)}, u32[]{:S(2)}, u32[]{:S(2)}) collective-permute-start(f32[32,1024]{1,0:T(8,128)S(1)} %shard_map.152.refs_2_.refs_0_), channel_id=1, source_target_pairs={{0,128},{16,144},{32,160},{48,176},{64,192},{80,208},{96,224},{112... | collective-permute-start | bytes 393224 | tf_op jit(solution)/shard_map/ppermute | solution.py:45
  68.4 32.1 %collective-permute-start.13 = (bf16[256,4096]{1,0:T(8,128)(2,1)S(1)}, bf16[256,4096]{1,0:T(8,128)(2,1)S(1)}, u32[]{:S(2)}, u32[]{:S(2)}) collective-permute-start(bf16[256,4096]{1,0:T(8,128)(2,1)S(1)} %get-tuple-element.52), channel_id=1, source_target_pairs={{0,1},{1,0},{2,3},{3,2},{4,5},{5,4},{6,7},{7,6},{8,9},{9,8},{10,11... | collective-permute-start | bytes 6291464 | tf_op jit(solution)/shard_map/ppermute | solution.py:41
  68.5 27.6 %collective-permute-start.16 = (bf16[512,1024]{1,0:T(8,128)(2,1)S(1)}, bf16[512,1024]{1,0:T(8,128)(2,1)S(1)}, u32[]{:S(2)}, u32[]{:S(2)}) collective-permute-start(bf16[512,1024]{1,0:T(8,128)(2,1)S(1)} %get-tuple-element.38.refs_3_), channel_id=1, source_target_pairs={{0,8},{1,9},{2,10},{3,11},{4,12},{5,13},{6,14},{7,15},{8,0},{9,1},... | collective-permute-start | bytes 3145736 | tf_op jit(solution)/shard_map/ppermute | solution.py:41
  71.2 9.0 %collective-permute-start.14 = (bf16[32,1024]{1,0:T(8,128)(2,1)S(1)}, bf16[32,1024]{1,0:T(8,128)(2,1)S(1)}, u32[]{:S(2)}, u32[]{:S(2)}) collective-permute-start(bf16[32,1024]{1,0:T(8,128)(2,1)S(1)} %shard_map.154.refs_17_.refs_0_), channel_id=1, source_target_pairs={{0,64},{16,80},{32,96},{48,112},{64,0},{80,16},{96,32},{112,48},{1... | collective-permute-start | bytes 196616 | tf_op jit(solution)/shard_map/ppermute | solution.py:45
  80.8 18.3 %collective-permute-start.15 = (bf16[64,1024]{1,0:T(8,128)(2,1)S(1)}, bf16[64,1024]{1,0:T(8,128)(2,1)S(1)}, u32[]{:S(2)}, u32[]{:S(2)}) collective-permute-start(bf16[64,1024]{1,0:T(8,128)(2,1)S(1)} %shard_map.156.refs_5_.refs_0_), channel_id=1, source_target_pairs={{0,32},{16,48},{32,0},{48,16},{64,96},{80,112},{96,64},{112,80},{1... | collective-permute-start | bytes 393224 | tf_op jit(solution)/shard_map/ppermute | solution.py:45
  80.9 30.2 %collective-permute-start.17 = (bf16[256,1024]{1,0:T(8,128)(2,1)S(1)}, bf16[256,1024]{1,0:T(8,128)(2,1)S(1)}, u32[]{:S(2)}, u32[]{:S(2)}) collective-permute-start(bf16[256,1024]{1,0:T(8,128)(2,1)S(1)} %get-tuple-element.56), channel_id=1, source_target_pairs={{0,8},{1,9},{2,10},{3,11},{4,12},{5,13},{6,14},{7,15},{8,0},{9,1},... | collective-permute-start | bytes 1572872 | tf_op jit(solution)/shard_map/ppermute | solution.py:41
  81.9 29.2 %collective-permute-start.18 = (bf16[256,1024]{1,0:T(8,128)(2,1)S(1)}, bf16[256,1024]{1,0:T(8,128)(2,1)S(1)}, u32[]{:S(2)}, u32[]{:S(2)}) collective-permute-start(bf16[256,1024]{1,0:T(8,128)(2,1)S(1)} %shard_map.151.refs_2_), channel_id=1, source_target_pairs={{0,4},{1,5},{2,6},{3,7},{4,0},{5,1},{6,2},{7,3},{8,12},{9,13},{10,... | collective-permute-start | bytes 1572872 | tf_op jit(solution)/shard_map/ppermute | solution.py:41
  97.8 13.3 %collective-permute-start.19 = (bf16[256,1024]{1,0:T(8,128)(2,1)S(1)}, bf16[256,1024]{1,0:T(8,128)(2,1)S(1)}, u32[]{:S(2)}, u32[]{:S(2)}) collective-permute-start(bf16[256,1024]{1,0:T(8,128)(2,1)S(1)} %get-tuple-element.53.refs_2_), channel_id=1, source_target_pairs={{0,2},{1,3},{2,4},{3,5},{4,6},{5,7},{6,0},{7,1},{8,10},{9,11},{10,... | collective-permute-start | bytes 1572872 | tf_op jit(solution)/shard_map/ppermute | solution.py:41
  99.1 13.9 %collective-permute-start.20 = (bf16[256,1024]{1,0:T(8,128)(2,1)S(1)}, bf16[256,1024]{1,0:T(8,128)(2,1)S(1)}, u32[]{:S(2)}, u32[]{:S(2)}) collective-permute-start(bf16[256,1024]{1,0:T(8,128)(2,1)S(1)} %get-tuple-element.57), channel_id=1, source_target_pairs={{0,6},{1,7},{2,0},{3,1},{4,2},{5,3},{6,4},{7,5},{8,14},{9,15},{10,... | collective-permute-start | bytes 1572872 | tf_op jit(solution)/shard_map/ppermute | solution.py:41
  100.6 6.9 %collective-permute-start.21 = (bf16[128,1024]{1,0:T(8,128)(2,1)S(1)}, bf16[128,1024]{1,0:T(8,128)(2,1)S(1)}, u32[]{:S(2)}, u32[]{:S(2)}) collective-permute-start(bf16[128,1024]{1,0:T(8,128)(2,1)S(1)} %shard_map.158.refs_4_.refs_0_), channel_id=1, source_target_pairs={{0,16},{16,0},{32,48},{48,32},{64,80},{80,64},{96,112},{112,96},{1... | collective-permute-start | bytes 786440 | tf_op jit(solution)/shard_map/ppermute | solution.py:45
  (11 other events, 61.0 us)

commit v2 on v0

v2 whole, which is shorter than its diff:
```python
import functools
import jax
import jax.numpy as jnp
import numpy as np
from jax import lax
from jax.experimental import pallas as pl
from jax.experimental.pallas import tpu as pltpu
from jax.sharding import PartitionSpec as P

first_bias = 0.9999734386011124
second_bias = 0.9940794707796655
BF, F32 = jnp.bfloat16, jnp.float32
B = 256
KV = 1024
D = 4096
LIMIT = 14 * 2**20
NEAR_COST, USE_COST, FAR_COST = 1_000_000, 1_000_000, 8_000_000

RELATIVE = ((1, 1), (1, 3), (1, 2), (1, 0), (0, 1), (0, 3), (0, 2), (0, 0))


def places():
    table = np.zeros((16, 16), np.int32)
    for me in range(16):
        core, x, half = me % 2, me // 2 % 4, me // 8
        for k, (dh, dx) in enumerate(RELATIVE):
            first = (half ^ dh) * 8 + (x + dx) % 4 * 2
            table[me, k], table[me, 8 + k] = first + core, first + 1 - core
    return table


def send(name, value, dx=0, half=0, core=0):
    pairs = [
        (h * 8 + x * 2 + c, (h ^ half) * 8 + (x + dx) % 4 * 2 + (c ^ core))
        for h in range(2)
        for x in range(4)
        for c in range(2)
    ]
    with jax.named_scope(name):
        return lax.ppermute(value, "fsdp", pairs)


def swap(name, value, flip):
    with jax.named_scope(name):
        return lax.ppermute(value, "replica", [(r, r ^ flip) for r in range(16)])


def tdot(a, b):
    return lax.dot_general(a, b, (((0,), (0,)), ((), ())), preferred_element_type=F32)


def ndot(a, b):
    return lax.dot_general(a, b, (((1,), (1,)), ((), ())), preferred_element_type=F32)


ANY = pl.BlockSpec(memory_space=pl.ANY)


def once(spec, grid):
    if grid > 1 or spec.block_shape is None:
        return spec
    return pl.BlockSpec(spec.block_shape, spec.index_map, pipeline_mode=pl.Buffered(1))


class Steps:
    def __init__(self, scalars):
        self.scalars = scalars
        self.last = None

    def __call__(self, name, kernel, ins, outs, grid=1, cost=1000):
        arrays, specs, n = [a for a, _ in ins], [spec for _, spec in ins], len(ins)
        tied = self.last is not None
        if tied:
            arrays.append(self.last)
            specs.append(ANY)

        def run(s, *refs):
            kernel(s, *refs[:n], *refs[n + tied :])

        result = pl.pallas_call(
            run,
            name=name,
            out_shape=[jax.ShapeDtypeStruct(shape, dtype) for shape, dtype, _ in outs],
            grid_spec=pltpu.PrefetchScalarGridSpec(
                num_scalar_prefetch=1,
                grid=(grid,),
                in_specs=[once(spec, grid) for spec in specs],
                out_specs=[once(spec, grid) for _, _, spec in outs],
            ),
            compiler_params=pltpu.CompilerParams(vmem_limit_bytes=LIMIT),
            cost_estimate=pl.CostEstimate(flops=0, bytes_accessed=cost, transcendentals=0),
        )(self.scalars, *arrays)
        self.last = result[0]
        return result

    def after(self, value):
        return lax.optimization_barrier((value, self.last))[0]


def grad_kernel(s, h, ph, c, pc, *rest):
    out = rest[-1]
    out[...] = (tdot(h[...], c[...]) + tdot(ph[...], pc[...])).astype(BF)


def add_near_kernel(s, h, ph, c, pc, came, _, to_right, to_left):
    value = (tdot(h[...], c[...]) + tdot(ph[...], pc[...]) + came[...].astype(F32)).astype(BF)
    for k, out in enumerate((to_right, to_left)):

        @pl.when(pl.program_id(0) == k)
        def _(out=out):
            out[...] = value


def add_far_kernel(s, h, ph, c, pc, came, right, left, out, own):
    value = tdot(h[...], c[...]) + tdot(ph[...], pc[...]) + came[...].astype(F32)

    @pl.when(pl.program_id(0) == 0)
    def _():
        out[...] = value.astype(BF)

    @pl.when(pl.program_id(0) == 1)
    def _():
        own[...] = value + right[...].astype(F32) + left[...].astype(F32)


def adam_kernel(s, partial, came, w, m, v, nw, nm, nv):
    grad = partial[...] + came[...].astype(F32)
    first = 0.9 * m[...] + 0.1 * grad
    second = 0.95 * v[...] + 0.05 * grad * grad
    nm[...] = first
    nv[...] = second
    scaled = second * (1 / second_bias)
    root = scaled * lax.rsqrt(scaled)
    update = first * (1 / first_bias) / (root + 1e-08)
    old = w[...].astype(F32)
    nw[...] = (old - 0.003 * (update + 0.1 * old)).astype(BF)


def forward_kernel(s, wl, sl, wr, sr, to_right, to_left):
    to_right[:128] = wl[...]
    to_right[128:] = sl[...]
    to_left[:128] = wr[...]
    to_left[128:] = sr[...]


def use(hs, phs, c, pc, ws, gi, pgi):
    a = p = None
    for i, w in enumerate(ws):
        ta = jnp.dot(hs[i][...], w, preferred_element_type=F32)
        tp = jnp.dot(phs[i][...], w, preferred_element_type=F32)
        a, p = (ta, tp) if a is None else (a + ta, p + tp)
        cols = slice(i * B, (i + 1) * B)
        gi[:, cols] = ndot(c[...], w).astype(BF)
        pgi[:, cols] = ndot(pc[...], w).astype(BF)
    return a, p


NEAR, FAR = (7, 3, 5, 4), (1, 0, 6, 2)


def near_kernel(s, *refs):
    hs, phs, (c, pc), ws = refs[:4], refs[4:8], refs[8:10], refs[10:14]
    a, p, gi, pgi = refs[14:]
    a[...], p[...] = use(hs, phs, c, pc, [w[...] for w in ws], gi, pgi)


def far_kernel(s, *refs):
    hs, phs, (c, pc), (l, r, ll, rr) = refs[:4], refs[4:8], refs[8:10], refs[10:14]
    a0, p0, a, gi, pgi, terms = refs[14:]
    ws = [
        l[...],
        r[...],
        jnp.concatenate([ll[:128], rr[:128]], axis=0),
        jnp.concatenate([ll[128:], rr[128:]], axis=0),
    ]
    own, peer = use(hs, phs, c, pc, ws, gi, pgi)
    a[...] = a0[...] + own
    terms[...] = (p0[...] + peer).astype(BF)


def finish_kernel(s, a, gi0, gi1, got0, got1, terms, keys, out):
    keys[...] = (a[...] + terms[...].astype(F32)).astype(BF)
    for order, own, came in ((NEAR, gi0, got0), (FAR, gi1, got1)):
        for i, k in enumerate(order):
            cols = slice(i * B, (i + 1) * B)
            out[:, pl.ds(pl.multiple_of(s[k] * B, B), B)] = own[:, cols]
            out[:, pl.ds(pl.multiple_of(s[8 + k] * B, B), B)] = came[:, cols]


def merge_kernel(s, a, b, whole, momentum, new_global, new_momentum):
    odd = lax.axis_index("replica") % 2
    pseudo = jnp.where(odd == pl.program_id(0), a[...], b[...]) * (1 / 4096)
    after = 0.9 * momentum[...] + pseudo
    new_momentum[...] = after
    new_global[...] = whole[...] - 0.7 * (pseudo + 0.9 * after)


def trade(name, value, flip):
    return swap(name, value.astype(jnp.float16), flip)


def rounded(value):
    return lax.reduce_precision(value, 5, 10)


def body(hidden, key_weight, adam_first, adam_second, key_cotangent, frag_global, frag_momentum, frag_local):
    h, w, c = hidden[0], key_weight[0], key_cotangent[0]
    local = frag_local[0]
    full = (B, KV)

    ph = send("peer_hidden", h, core=1)
    pc = send("peer_cotangent", c, core=1)
    w_half = send("weight_half", w, half=1)
    w_left = send("weight_left", w, dx=1)
    w_right = send("weight_right", w, dx=3)
    f1 = swap("island1", local, 1)

    table = jnp.asarray(places())
    step = Steps(lax.dynamic_index_in_dim(table, lax.axis_index("fsdp"), keepdims=False))
    stay = lambda a: pltpu.with_memory_space_constraint(a, pltpu.HBM)
    h, c = stay(h), stay(c)

    def at(shape, row=0, col=0):
        pick = lambda p, k, s: p(k, s) if callable(p) else p
        return pl.BlockSpec(shape, lambda k, s: (pick(row, k, s), pick(col, k, s)))

    def rows(n, row=0):
        return at((n, KV), row)

    def blocks(base):
        column = at((B, B), 0, lambda k, s: s[base + k])
        return [(h, column), (ph, column), (c, at(full)), (pc, at(full))]

    def chosen(order):
        picks = [at((B, B), 0, lambda _, s, k=k: s[k]) for k in order]
        return [(h, p) for p in picks] + [(ph, p) for p in picks] + [(c, at(full)), (pc, at(full))]

    two = rows(B, lambda k, s: k)
    pair = [(full, BF, at(full))] * 2

    (out,) = step("grad_near", grad_kernel, blocks(0), [((2 * B, KV), BF, two)], grid=2)
    y_near = send("half_near", out, half=1)
    (out,) = step("grad_far", grad_kernel, blocks(2) + [(a, ANY) for a in (w_left, w_right)], [((2 * B, KV), BF, two)], grid=2)
    y_far = send("half_far", out, half=1)
    w_half = step.after(w_half)
    s2l = send("second_left", w_half, dx=1)
    s2r = send("second_right", w_half, dx=3)

    odd = lax.axis_index("replica") % 2
    mine = lambda a: lax.dynamic_slice_in_dim(a, odd * 128, 128)
    difference = (mine(frag_global) * 2 - mine(local).astype(F32) - mine(step.after(f1)).astype(F32)) * 256
    step.last = total = rounded(difference)
    f2 = trade("island2", total, 2)

    acc_a, acc_p, gi0, pgi0 = step(
        "near",
        near_kernel,
        chosen(NEAR) + [(a, at(full)) for a in (w, w_half, w_left, w_right)],
        [(full, F32, at(full))] * 2 + [(full, BF, at(full))] * 2,
    )
    got0 = send("got_near", pgi0, core=1)
    to_right, to_left = step(
        "forward",
        forward_kernel,
        [(w_left, rows(128)), (s2l, rows(128)), (w_right, rows(128, 1)), (s2r, rows(128, 1))],
        pair,
    )
    s3l = send("third_left", to_right, dx=1)
    s3r = send("third_right", to_left, dx=3)

    def summed(name, total, came, flip):
        step.last = total = rounded(total + step.after(came).astype(F32))
        return total, trade(name, total, flip)

    to_right, to_left = step(
        "add_near", add_near_kernel, blocks(4) + [(y_near, two), (got0, ANY)], pair, grid=2, cost=NEAR_COST
    )
    x1 = send("along_right", to_right, dx=1)
    x3 = send("along_left", to_left, dx=3)
    total, f3 = summed("island3", total, f2, 6)
    f3, s3l, s3r = lax.optimization_barrier((f3, s3l, s3r))
    total, f4 = summed("island4", total, f3, 8)

    out, partial = step(
        "add_far",
        add_far_kernel,
        blocks(6) + [(y_far, two), (x1, at(full)), (x3, at(full))],
        [(full, BF, at(full)), (full, F32, at(full))],
        grid=2,
        cost=FAR_COST,
    )
    x2 = send("along_two", out, dx=2)

    acc, gi1, pgi1, terms = step(
        "far",
        far_kernel,
        chosen(FAR) + [(a, at(full)) for a in (s2l, s2r, s3l, s3r, acc_a, acc_p)],
        [(full, F32, at(full))] + [(full, BF, at(full))] * 3,
        cost=USE_COST,
    )
    got1 = send("got_far", pgi1, core=1)
    got2 = send("got_terms", terms, core=1)

    total, f5 = summed("island5", total, f4, 1)

    keys, input_grad = step(
        "finish",
        finish_kernel,
        [(a, at(full)) for a in (acc, gi0, gi1, got0, got1, got2)],
        [(full, BF, at(full)), ((B, D), BF, at((B, D)))],
    )
    tile = rows(64, lambda k, s: k)
    new_weight, new_first, new_second = step(
        "adam",
        adam_kernel,
        [(stay(a), tile) for a in (partial, x2, w, adam_first[0], adam_second[0])],
        [(full, BF, tile), (full, F32, tile), (full, F32, tile)],
        grid=4,
    )
    half = rows(128, lambda k, s: k)
    new_global, new_momentum = step(
        "merge",
        merge_kernel,
        [(total, rows(128)), (step.after(f5).astype(F32), rows(128))]
        + [(stay(a), half) for a in (frag_global, frag_momentum)],
        [(full, F32, half)] * 2,
        grid=2,
    )
    return (
        keys[None],
        input_grad[None],
        new_weight[None],
        new_first[None],
        new_second[None],
        new_global,
        new_momentum,
    )


def solution(mesh):
    rows = P("replica", "fsdp", None)
    return jax.shard_map(
        body,
        mesh=mesh,
        in_specs=(rows,) * 5 + (P("fsdp", None),) * 2 + (rows,),
        out_specs=(rows,) * 5 + (P("fsdp", None),) * 2,
        check_vma=False,
    )
```

time: 231 us -> 96.4 us (0.42); the launches traced: 227 us -> 95.5 us
  waiting for transfers between devices: 184 us -> 19.4 us
  starting transfers between devices: 0.13 us -> 35.8 us
  Pallas kernels: 0 us -> 32.6 us
  matrix products: 17.2 us -> 0 us
  between operations: 15.5 us -> 0.81 us
  other arithmetic: 10.2 us -> 2.28 us
  local copies, waits for them, and re-layouts: 0.02 us -> 4.54 us
    psum x1 -> x0, waiting for transfers between devices: 135 us -> none  [body(): summed = lax.psum(pseudo_terms, 'replica')]
    all_gather x1 -> x0, waiting for transfers between devices: 49.2 us -> none  [body(): whole = lax.all_gather(weight, 'fsdp', axis=0, tiled=True)]
    ppermute x0 -> x22, starting transfers between devices: none -> 35.8 us  [the longest x17 20.5 us: send(): return lax.ppermute(value, 'fsdp', pairs)]
    pallas_call x0 -> x10, Pallas kernels: none -> 32.6 us  [__call__(): pl.pallas_call(run, name=name, out_shape=[jax.ShapeDtypeStruct(shape, dty...]
    ppermute x0 -> x22, waiting for transfers between devices: none -> 19.4 us  [the longest x17 12.9 us: send(): return lax.ppermute(value, 'fsdp', pairs)]
    dot_general x3 -> x0, matrix products: 17.2 us -> none  [the longest x1 6.74 us: body(): lax.dot_general(inputs, cotangent, (((0,), (0,)), ((), ())), preferred_el...]
    sub x2 -> x0, other arithmetic: 5.97 us -> none  [the longest x1 3.32 us: body(): new_global = frag_global - 0.7 * (pseudo + 0.9 * new_momentum)]
    broadcast_in_dim x1 -> x0, other arithmetic: 4.25 us -> none  [body(): new_second[None]]
  transfers between devices with their start and end apart: 3 -> 22, of which waited for: 2 -> 9; matrix products, arithmetic and copies ran while one was open for 6% -> 3% of each run, Pallas kernels for 0% -> 31%
where the time goes in v2:
time: 96.4 us; the launch traced here: 95.5 us
  starting transfers between devices  35.8 us (37%)
  Pallas kernels  32.6 us (34%)
  waiting for transfers between devices  19.4 us (20%)
  local copies, waits for them, and re-layouts  4.54 us (5%)
  other arithmetic  2.28 us (2%)
    pallas_call x10, Pallas kernels, __call__(): pl.pallas_call(run, name=name, out_shape=[jax.ShapeDtypeStruct(shape, dty...  32.6 us
    ppermute x17, starting transfers between devices, send(): return lax.ppermute(value, 'fsdp', pairs)  20.5 us
    ppermute x5, starting transfers between devices, swap(): return lax.ppermute(value, 'replica', [(r, r ^ flip) for r in range(16)])  15.3 us
    ppermute x17, waiting for transfers between devices, send(): return lax.ppermute(value, 'fsdp', pairs)  12.9 us
    ppermute x5, waiting for transfers between devices, swap(): return lax.ppermute(value, 'replica', [(r, r ^ flip) for r in range(16)])  6.51 us
    unnamed x14, local copies, waits for them, and re-layouts  3.85 us
    convert_element_type x4, other arithmetic, trade(): return swap(name, value.astype(jnp.float16), flip)  2.25 us
  transfers between devices with their start and end apart: 22, of which 9 were waited for; matrix products, arithmetic and copies ran while one was open for 3% of the time, Pallas kernels for 31%

profile of v2, /device:TPU:6, one launch (start us, length us, event | category | flops | bytes accessed | tf_op | source)
XLA Modules:
  0.0 95.5 jit_solution(16947268014864577850)
XLA Ops:
  2.1 2.4 %collective-permute-start.3 = (bf16[256,1024]{1,0:T(8,128)(2,1)}, bf16[256,1024]{1,0:T(8,128)(2,1)}, u32[]{:S(2)}, u32[]{:S(2)}) collective-permute-start(bf16[256,1024]{1,0:T(8,128)(2,1)} %bitcast.18), channel_id=1, source_target_pairs={{0,2},{1,3},{2,4},{3,5},{4,6},{5,7},{6,0},{7,1},{8,10},{9,11},{10,... | collective-permute-start | bytes 1572872 | tf_op jit(solution)/shard_map/weight_left/ppermute | solution.py:40
  4.5 3.2 %collective-permute-start.2 = (bf16[256,1024]{1,0:T(8,128)(2,1)}, bf16[256,1024]{1,0:T(8,128)(2,1)}, u32[]{:S(2)}, u32[]{:S(2)}) collective-permute-start(bf16[256,1024]{1,0:T(8,128)(2,1)} %bitcast.19), channel_id=1, source_target_pairs={{0,8},{1,9},{2,10},{3,11},{4,12},{5,13},{6,14},{7,15},{8,0},{9,1},... | collective-permute-start | bytes 1572872 | tf_op jit(solution)/shard_map/weight_half/ppermute | solution.py:40
  7.7 1.9 %collective-permute-start.7 = (bf16[256,1024]{1,0:T(8,128)(2,1)}, bf16[256,1024]{1,0:T(8,128)(2,1)}, u32[]{:S(2)}, u32[]{:S(2)}) collective-permute-start(bf16[256,1024]{1,0:T(8,128)(2,1)} %bitcast.46), channel_id=1, source_target_pairs={{0,16},{16,0},{32,48},{48,32},{64,80},{80,64},{96,112},{112,96},{1... | collective-permute-start | bytes 1572872 | tf_op jit(solution)/shard_map/island1/ppermute | solution.py:45
  10.3 3.4 %grad_near.1.refs_6_ = bf16[512,1024]{1,0:T(8,128)(2,1)} custom-call(s32[16]{0:T(128)S(1)} %fusion.3.s, bf16[256,4096]{1,0:T(8,128)(2,1)} %bitcast.25, bf16[256,4096]{1,0:T(8,128)(2,1)S(1)} %collective-permute-done.refs_1_.refs_4_.refs_5_.refs_6_.refs_7_, bf16[256,1024]{1,0:T(8,128)(2,1)} %bitcast.38, ...), custom_call_target="tpu_custom_call" | custom-call | bytes 1000 | tf_op jit(solution)/shard_map/grad_near/pallas_call | solution.py:80
  16.6 2.6 %grad_far.1 = bf16[512,1024]{1,0:T(8,128)(2,1)S(1)} custom-call(s32[16]{0:T(128)S(1)} %fusion.3.s, bf16[256,4096]{1,0:T(8,128)(2,1)} %bitcast.26, bf16[256,4096]{1,0:T(8,128)(2,1)S(1)} %collective-permute-done.refs_1_.refs_4_.refs_5_.refs_6_.refs_7_, bf16[256,1024]{1,0:T(8,128)(2,1)} %bitcast.39, ...), custom_call_target="tpu_custom_call" | custom-call | bytes 1000 | tf_op jit(solution)/shard_map/grad_far/pallas_call | solution.py:80
  19.2 1.9 %collective-permute-done.2.refs_11_ = bf16[256,1024]{1,0:T(8,128)(2,1)} collective-permute-done((bf16[256,1024]{1,0:T(8,128)(2,1)}, bf16[256,1024]{1,0:T(8,128)(2,1)}, u32[]{:S(2)}, u32[]{:S(2)}) %collective-permute-start.2) | collective-permute-done | bytes 524320 | tf_op jit(solution)/shard_map/weight_half/ppermute | solution.py:40
  21.1 3.2 %collective-permute-start.5 = (bf16[256,1024]{1,0:T(8,128)(2,1)}, bf16[256,1024]{1,0:T(8,128)(2,1)S(1)}, u32[]{:S(2)}, u32[]{:S(2)}) collective-permute-start(bf16[256,1024]{1,0:T(8,128)(2,1)} %collective-permute-done.2.refs_11_), channel_id=1, source_target_pairs={{0,2},{1,3},{2,4},{3,5},{4,6},{5,7},{6,0},{7,1},{8,10},{9,11},{10,... | collective-permute-start | bytes 1572872 | tf_op jit(solution)/shard_map/second_left/ppermute | solution.py:40
  25.7 4.5 %near.1 = (f32[256,1024]{1,0:T(8,128)S(1)}, f32[256,1024]{1,0:T(8,128)S(1)}, bf16[256,1024]{1,0:T(8,128)(2,1)S(1)}, bf16[256,1024]{1,0:T(8,128)(2,1)S(1)}) custom-call(s32[16]{0:T(128)S(1)} %fusion.3.s, bf16[256,4096]{1,0:T(8,128)(2,1)} %bitcast.27, bf16[256,4096]{1,0:T(8,128)(2,1)} %bitcast.28, bf16[256,4096]{1,0:T(8,128)(2,1)} %bitcast.29, ...), custom_call_target="tpu_custom_call" | custom-call | bytes 1000 | tf_op jit(solution)/shard_map/near/pallas_call | solution.py:80
  30.4 3.4 %collective-permute-start.8 = (f16[128,1024]{1,0:T(8,128)(2,1)S(1)}, f16[128,1024]{1,0:T(8,128)(2,1)S(1)}, u32[]{:S(2)}, u32[]{:S(2)}) collective-permute-start(f16[128,1024]{1,0:T(8,128)(2,1)S(1)} %get-tuple-element.73), channel_id=1, source_target_pairs={{0,32},{16,48},{32,0},{48,16},{64,96},{80,112},{96,64},{112,80},{1... | collective-permute-start | bytes 786440 | tf_op jit(solution)/shard_map/island2/ppermute | solution.py:45
  34.0 3.1 %collective-permute-start.14 = (bf16[512,1024]{1,0:T(8,128)(2,1)S(1)}, bf16[512,1024]{1,0:T(8,128)(2,1)S(1)}, u32[]{:S(2)}, u32[]{:S(2)}) collective-permute-start(bf16[512,1024]{1,0:T(8,128)(2,1)S(1)} %grad_far.1), channel_id=1, source_target_pairs={{0,8},{1,9},{2,10},{3,11},{4,12},{5,13},{6,14},{7,15},{8,0},{9,1},... | collective-permute-start | bytes 3145736 | tf_op jit(solution)/shard_map/half_far/ppermute | solution.py:40
  38.7 3.2 %collective-permute-start.12 = (bf16[256,1024]{1,0:T(8,128)(2,1)S(1)}, bf16[256,1024]{1,0:T(8,128)(2,1)S(1)}, u32[]{:S(2)}, u32[]{:S(2)}) collective-permute-start(bf16[256,1024]{1,0:T(8,128)(2,1)S(1)} %get-tuple-element.41.refs_6_), channel_id=1, source_target_pairs={{0,2},{1,3},{2,4},{3,5},{4,6},{5,7},{6,0},{7,1},{8,10},{9,11},{10,... | collective-permute-start | bytes 1572872 | tf_op jit(solution)/shard_map/third_left/ppermute | solution.py:40
  41.9 1.7 %collective-permute-done.9.refs_4_ = bf16[512,1024]{1,0:T(8,128)(2,1)} collective-permute-done((bf16[512,1024]{1,0:T(8,128)(2,1)}, bf16[512,1024]{1,0:T(8,128)(2,1)}, u32[]{:S(2)}, u32[]{:S(2)}) %collective-permute-start.9) | collective-permute-done | bytes 1048608 | tf_op jit(solution)/shard_map/half_near/ppermute | solution.py:40
  43.6 2.9 %add_near.1 = (bf16[256,1024]{1,0:T(8,128)(2,1)S(1)}, bf16[256,1024]{1,0:T(8,128)(2,1)S(1)}) custom-call(s32[16]{0:T(128)S(1)} %fusion.3.s, bf16[256,4096]{1,0:T(8,128)(2,1)} %bitcast.31, bf16[256,4096]{1,0:T(8,128)(2,1)S(1)} %collective-permute-done.refs_1_.refs_4_.refs_5_.refs_6_.refs_7_, bf16[256,1024]{1,0:T(8,128)(2,1)} %bitcast.41, ...), custom_call_target="tpu_custom_call" | custom-call | bytes 1000000 | tf_op jit(solution)/shard_map/add_near/pallas_call | solution.py:80
  46.9 6.4 %collective-permute-start.11 = (f16[128,1024]{1,0:T(8,128)(2,1)S(1)}, f16[128,1024]{1,0:T(8,128)(2,1)S(1)}, u32[]{:S(2)}, u32[]{:S(2)}) collective-permute-start(f16[128,1024]{1,0:T(8,128)(2,1)S(1)} %get-tuple-element.71), channel_id=1, source_target_pairs={{0,96},{16,112},{32,64},{48,80},{64,32},{80,48},{96,0},{112,16},{1... | collective-permute-start | bytes 786440 | tf_op jit(solution)/shard_map/island3/ppermute | solution.py:45
  53.5 1.8 %collective-permute-start.16 = (bf16[256,1024]{1,0:T(8,128)(2,1)S(1)}, bf16[256,1024]{1,0:T(8,128)(2,1)S(1)}, u32[]{:S(2)}, u32[]{:S(2)}) collective-permute-start(bf16[256,1024]{1,0:T(8,128)(2,1)S(1)} %get-tuple-element.48), channel_id=1, source_target_pairs={{0,6},{1,7},{2,0},{3,1},{4,2},{5,3},{6,4},{7,5},{8,14},{9,15},{10,... | collective-permute-start | bytes 1572872 | tf_op jit(solution)/shard_map/along_left/ppermute | solution.py:40
  55.3 6.5 %collective-permute-done.11 = f16[128,1024]{1,0:T(8,128)(2,1)S(1)} collective-permute-done((f16[128,1024]{1,0:T(8,128)(2,1)S(1)}, f16[128,1024]{1,0:T(8,128)(2,1)S(1)}, u32[]{:S(2)}, u32[]{:S(2)}) %collective-permute-start.11) | collective-permute-done | bytes 262176 | tf_op jit(solution)/shard_map/island3/ppermute | solution.py:45
  65.2 2.2 %collective-permute-done.16.refs_6_ = bf16[256,1024]{1,0:T(8,128)(2,1)S(1)} collective-permute-done((bf16[256,1024]{1,0:T(8,128)(2,1)S(1)}, bf16[256,1024]{1,0:T(8,128)(2,1)S(1)}, u32[]{:S(2)}, u32[]{:S(2)}) %collective-permute-start.16) | collective-permute-done | bytes 524320 | tf_op jit(solution)/shard_map/along_left/ppermute | solution.py:40
  67.4 2.8 %add_far.1 = (bf16[256,1024]{1,0:T(8,128)(2,1)S(1)}, f32[256,1024]{1,0:T(8,128)S(1)}) custom-call(s32[16]{0:T(128)S(1)} %fusion.3.s, bf16[256,4096]{1,0:T(8,128)(2,1)} %bitcast.32, bf16[256,4096]{1,0:T(8,128)(2,1)S(1)} %collective-permute-done.refs_1_.refs_4_.refs_5_.refs_6_.refs_7_, bf16[256,1024]{1,0:T(8,128)(2,1)} %bitcast.42, ...), custom_call_target="tpu_custom_call" | custom-call | bytes 8000000 | tf_op jit(solution)/shard_map/add_far/pallas_call | solution.py:80
  71.2 4.3 %far.1 = (f32[256,1024]{1,0:T(8,128)S(1)}, bf16[256,1024]{1,0:T(8,128)(2,1)S(1)}, bf16[256,1024]{1,0:T(8,128)(2,1)S(1)}, bf16[256,1024]{1,0:T(8,128)(2,1)S(1)}) custom-call(s32[16]{0:T(128)S(1)} %fusion.3.s, bf16[256,4096]{1,0:T(8,128)(2,1)} %bitcast.33, bf16[256,4096]{1,0:T(8,128)(2,1)} %bitcast.34, bf16[256,4096]{1,0:T(8,128)(2,1)} %bitcast.35, ...), custom_call_target="tpu_custom_call" | custom-call | bytes 1000000 | tf_op jit(solution)/shard_map/far/pallas_call | solution.py:80
  76.4 2.0 %collective-permute-start.21 = (f16[128,1024]{1,0:T(8,128)(2,1)S(1)}, f16[128,1024]{1,0:T(8,128)(2,1)S(1)}, u32[]{:S(2)}, u32[]{:S(2)}) collective-permute-start(f16[128,1024]{1,0:T(8,128)(2,1)S(1)} %get-tuple-element.67), channel_id=1, source_target_pairs={{0,16},{16,0},{32,48},{48,32},{64,80},{80,64},{96,112},{112,96},{1... | collective-permute-start | bytes 786440 | tf_op jit(solution)/shard_map/island5/ppermute | solution.py:45
  78.4 2.4 %finish.1 = (bf16[256,1024]{1,0:T(8,128)(2,1)}, bf16[256,4096]{1,0:T(8,128)(2,1)}) custom-call(s32[16]{0:T(128)S(1)} %fusion.3.s, f32[256,1024]{1,0:T(8,128)S(1)} %get-tuple-element.52.refs_0_, bf16[256,1024]{1,0:T(8,128)(2,1)S(1)} %get-tuple-element.53.refs_1_, bf16[256,1024]{1,0:T(8,128)(2,1)S(1)} %get-tuple-element.54.refs_2_, ...), custom_call_target="tpu_custom_call" | custom-call | bytes 1000 | tf_op jit(solution)/shard_map/finish/pallas_call | solution.py:80
  80.8 3.7 %collective-permute-done.20.refs_1_ = bf16[256,1024]{1,0:T(8,128)(2,1)S(1)} collective-permute-done((bf16[256,1024]{1,0:T(8,128)(2,1)S(1)}, bf16[256,1024]{1,0:T(8,128)(2,1)S(1)}, u32[]{:S(2)}, u32[]{:S(2)}) %collective-permute-start.20) | collective-permute-done | bytes 524320 | tf_op jit(solution)/shard_map/along_two/ppermute | solution.py:40
  86.3 4.8 %adam.1 = (bf16[256,1024]{1,0:T(8,128)(2,1)}, f32[256,1024]{1,0:T(8,128)}, f32[256,1024]{1,0:T(8,128)}) custom-call(s32[16]{0:T(128)S(1)} %fusion.3.s, f32[256,1024]{1,0:T(8,128)} %copy-done.1, bf16[256,1024]{1,0:T(8,128)(2,1)} %copy-done.5, bf16[256,1024]{1,0:T(8,128)(2,1)} %bitcast.20, f32[256,1024]{1,0:T(8,128)} %bitcast.44, f32[256,1024]{1,0:T(8,128)} %bitcast.45, ...), custom_call_target="tpu_custom_call" | custom-call | bytes 1000 | tf_op jit(solution)/shard_map/adam/pallas_call | solution.py:80
  92.2 3.2 %merge.1 = (f32[256,1024]{1,0:T(8,128)}, f32[256,1024]{1,0:T(8,128)}) custom-call(s32[16]{0:T(128)S(1)} %fusion.3.s, f32[128,1024]{1,0:T(8,128)S(1)} %get-tuple-element.68.refs_6_.refs_0_, f32[128,1024]{1,0:T(8,128)S(1)} %convert_element_type.43.refs_1_, f32[256,1024]{1,0:T(8,128)} %refs_2_.1, f32[256,1024]{1,0:T(8,128)} %refs_3_.1, ...), custom_call_target="tpu_custom_call" | custom-call | bytes 1000 | tf_op jit(solution)/shard_map/merge/pallas_call | solution.py:80
  (50 shorter events, 17.0 us)
Async XLA Ops:
  0.6 9.6 %collective-permute-start = (bf16[256,4096]{1,0:T(8,128)(2,1)}, bf16[256,4096]{1,0:T(8,128)(2,1)S(1)}, u32[]{:S(2)}, u32[]{:S(2)}) collective-permute-start(bf16[256,4096]{1,0:T(8,128)(2,1)} %bitcast.24), channel_id=1, source_target_pairs={{0,1},{1,0},{2,3},{3,2},{4,5},{5,4},{6,7},{7,6},{8,9},{9,8},{10,11... | collective-permute-start | bytes 6291464 | tf_op jit(solution)/shard_map/peer_hidden/ppermute | solution.py:40
  0.7 6.9 %collective-permute-start.1 = (bf16[256,1024]{1,0:T(8,128)(2,1)}, bf16[256,1024]{1,0:T(8,128)(2,1)S(1)}, u32[]{:S(2)}, u32[]{:S(2)}) collective-permute-start(bf16[256,1024]{1,0:T(8,128)(2,1)} %bitcast.37), channel_id=1, source_target_pairs={{0,1},{1,0},{2,3},{3,2},{4,5},{5,4},{6,7},{7,6},{8,9},{9,8},{10,11... | collective-permute-start | bytes 1572872 | tf_op jit(solution)/shard_map/peer_cotangent/ppermute | solution.py:40
  1.2 15.4 %collective-permute-start.4 = (bf16[256,1024]{1,0:T(8,128)(2,1)}, bf16[256,1024]{1,0:T(8,128)(2,1)S(1)}, u32[]{:S(2)}, u32[]{:S(2)}) collective-permute-start(bf16[256,1024]{1,0:T(8,128)(2,1)} %bitcast.17), channel_id=1, source_target_pairs={{0,6},{1,7},{2,0},{3,1},{4,2},{5,3},{6,4},{7,5},{8,14},{9,15},{10,... | collective-permute-start | bytes 1572872 | tf_op jit(solution)/shard_map/weight_right/ppermute | solution.py:40
  2.1 14.5 %collective-permute-start.3 = (bf16[256,1024]{1,0:T(8,128)(2,1)}, bf16[256,1024]{1,0:T(8,128)(2,1)}, u32[]{:S(2)}, u32[]{:S(2)}) collective-permute-start(bf16[256,1024]{1,0:T(8,128)(2,1)} %bitcast.18), channel_id=1, source_target_pairs={{0,2},{1,3},{2,4},{3,5},{4,6},{5,7},{6,0},{7,1},{8,10},{9,11},{10,... | collective-permute-start | bytes 1572872 | tf_op jit(solution)/shard_map/weight_left/ppermute | solution.py:40
  4.5 16.7 %collective-permute-start.2 = (bf16[256,1024]{1,0:T(8,128)(2,1)}, bf16[256,1024]{1,0:T(8,128)(2,1)}, u32[]{:S(2)}, u32[]{:S(2)}) collective-permute-start(bf16[256,1024]{1,0:T(8,128)(2,1)} %bitcast.19), channel_id=1, source_target_pairs={{0,8},{1,9},{2,10},{3,11},{4,12},{5,13},{6,14},{7,15},{8,0},{9,1},... | collective-permute-start | bytes 1572872 | tf_op jit(solution)/shard_map/weight_half/ppermute | solution.py:40
  7.7 16.7 %collective-permute-start.7 = (bf16[256,1024]{1,0:T(8,128)(2,1)}, bf16[256,1024]{1,0:T(8,128)(2,1)}, u32[]{:S(2)}, u32[]{:S(2)}) collective-permute-start(bf16[256,1024]{1,0:T(8,128)(2,1)} %bitcast.46), channel_id=1, source_target_pairs={{0,16},{16,0},{32,48},{48,32},{64,80},{80,64},{96,112},{112,96},{1... | collective-permute-start | bytes 1572872 | tf_op jit(solution)/shard_map/island1/ppermute | solution.py:45
  13.7 29.9 %collective-permute-start.9 = (bf16[512,1024]{1,0:T(8,128)(2,1)}, bf16[512,1024]{1,0:T(8,128)(2,1)}, u32[]{:S(2)}, u32[]{:S(2)}) collective-permute-start(bf16[512,1024]{1,0:T(8,128)(2,1)} %grad_near.1.refs_6_), channel_id=1, source_target_pairs={{0,8},{1,9},{2,10},{3,11},{4,12},{5,13},{6,14},{7,15},{8,0},{9,1},... | collective-permute-start | bytes 3145736 | tf_op jit(solution)/shard_map/half_near/ppermute | solution.py:40
  15.1 9.3 %copy-start.4 = (f32[256,1024]{1,0:T(8,128)S(1)}, f32[256,1024]{1,0:T(8,128)}, u32[]{:S(2)}) copy-start(f32[256,1024]{1,0:T(8,128)} %refs_2_.1) | copy-start | bytes 3145732
  15.1 9.3 %copy-start.6 = (bf16[1,256,1024]{2,1,0:T(8,128)(2,1)S(1)}, bf16[1,256,1024]{2,1,0:T(8,128)(2,1)}, u32[]{:S(2)}) copy-start(bf16[1,256,1024]{2,1,0:T(8,128)(2,1)} %param.16) | copy-start | bytes 1572868
  21.1 12.8 %collective-permute-start.6 = (bf16[256,1024]{1,0:T(8,128)(2,1)}, bf16[256,1024]{1,0:T(8,128)(2,1)S(1)}, u32[]{:S(2)}, u32[]{:S(2)}) collective-permute-start(bf16[256,1024]{1,0:T(8,128)(2,1)} %collective-permute-done.2.refs_11_), channel_id=1, source_target_pairs={{0,6},{1,7},{2,0},{3,1},{4,2},{5,3},{6,4},{7,5},{8,14},{9,15},{10,... | collective-permute-start | bytes 1572872 | tf_op jit(solution)/shard_map/second_right/ppermute | solution.py:40
  21.1 15.9 %collective-permute-start.5 = (bf16[256,1024]{1,0:T(8,128)(2,1)}, bf16[256,1024]{1,0:T(8,128)(2,1)S(1)}, u32[]{:S(2)}, u32[]{:S(2)}) collective-permute-start(bf16[256,1024]{1,0:T(8,128)(2,1)} %collective-permute-done.2.refs_11_), channel_id=1, source_target_pairs={{0,2},{1,3},{2,4},{3,5},{4,6},{5,7},{6,0},{7,1},{8,10},{9,11},{10,... | collective-permute-start | bytes 1572872 | tf_op jit(solution)/shard_map/second_left/ppermute | solution.py:40
  30.3 8.4 %collective-permute-start.10 = (bf16[256,1024]{1,0:T(8,128)(2,1)S(1)}, bf16[256,1024]{1,0:T(8,128)(2,1)S(1)}, u32[]{:S(2)}, u32[]{:S(2)}) collective-permute-start(bf16[256,1024]{1,0:T(8,128)(2,1)S(1)} %get-tuple-element.39), channel_id=1, source_target_pairs={{0,1},{1,0},{2,3},{3,2},{4,5},{5,4},{6,7},{7,6},{8,9},{9,8},{10,11... | collective-permute-start | bytes 1572872 | tf_op jit(solution)/shard_map/got_near/ppermute | solution.py:40
  30.4 16.2 %collective-permute-start.8 = (f16[128,1024]{1,0:T(8,128)(2,1)S(1)}, f16[128,1024]{1,0:T(8,128)(2,1)S(1)}, u32[]{:S(2)}, u32[]{:S(2)}) collective-permute-start(f16[128,1024]{1,0:T(8,128)(2,1)S(1)} %get-tuple-element.73), channel_id=1, source_target_pairs={{0,32},{16,48},{32,0},{48,16},{64,96},{80,112},{96,64},{112,80},{1... | collective-permute-start | bytes 786440 | tf_op jit(solution)/shard_map/island2/ppermute | solution.py:45
  34.0 31.2 %collective-permute-start.14 = (bf16[512,1024]{1,0:T(8,128)(2,1)S(1)}, bf16[512,1024]{1,0:T(8,128)(2,1)S(1)}, u32[]{:S(2)}, u32[]{:S(2)}) collective-permute-start(bf16[512,1024]{1,0:T(8,128)(2,1)S(1)} %grad_far.1), channel_id=1, source_target_pairs={{0,8},{1,9},{2,10},{3,11},{4,12},{5,13},{6,14},{7,15},{8,0},{9,1},... | collective-permute-start | bytes 3145736 | tf_op jit(solution)/shard_map/half_far/ppermute | solution.py:40
  38.6 14.9 %collective-permute-start.13 = (bf16[256,1024]{1,0:T(8,128)(2,1)S(1)}, bf16[256,1024]{1,0:T(8,128)(2,1)S(1)}, u32[]{:S(2)}, u32[]{:S(2)}) collective-permute-start(bf16[256,1024]{1,0:T(8,128)(2,1)S(1)} %get-tuple-element.44), channel_id=1, source_target_pairs={{0,6},{1,7},{2,0},{3,1},{4,2},{5,3},{6,4},{7,5},{8,14},{9,15},{10,... | collective-permute-start | bytes 1572872 | tf_op jit(solution)/shard_map/third_right/ppermute | solution.py:40
  38.7 16.6 %collective-permute-start.12 = (bf16[256,1024]{1,0:T(8,128)(2,1)S(1)}, bf16[256,1024]{1,0:T(8,128)(2,1)S(1)}, u32[]{:S(2)}, u32[]{:S(2)}) collective-permute-start(bf16[256,1024]{1,0:T(8,128)(2,1)S(1)} %get-tuple-element.41.refs_6_), channel_id=1, source_target_pairs={{0,2},{1,3},{2,4},{3,5},{4,6},{5,7},{6,0},{7,1},{8,10},{9,11},{10,... | collective-permute-start | bytes 1572872 | tf_op jit(solution)/shard_map/third_left/ppermute | solution.py:40
  46.9 14.9 %collective-permute-start.11 = (f16[128,1024]{1,0:T(8,128)(2,1)S(1)}, f16[128,1024]{1,0:T(8,128)(2,1)S(1)}, u32[]{:S(2)}, u32[]{:S(2)}) collective-permute-start(f16[128,1024]{1,0:T(8,128)(2,1)S(1)} %get-tuple-element.71), channel_id=1, source_target_pairs={{0,96},{16,112},{32,64},{48,80},{64,32},{80,48},{96,0},{112,16},{1... | collective-permute-start | bytes 786440 | tf_op jit(solution)/shard_map/island3/ppermute | solution.py:45
  53.3 14.1 %collective-permute-start.15 = (bf16[256,1024]{1,0:T(8,128)(2,1)S(1)}, bf16[256,1024]{1,0:T(8,128)(2,1)S(1)}, u32[]{:S(2)}, u32[]{:S(2)}) collective-permute-start(bf16[256,1024]{1,0:T(8,128)(2,1)S(1)} %get-tuple-element.42), channel_id=1, source_target_pairs={{0,2},{1,3},{2,4},{3,5},{4,6},{5,7},{6,0},{7,1},{8,10},{9,11},{10,... | collective-permute-start | bytes 1572872 | tf_op jit(solution)/shard_map/along_right/ppermute | solution.py:40
  53.5 13.9 %collective-permute-start.16 = (bf16[256,1024]{1,0:T(8,128)(2,1)S(1)}, bf16[256,1024]{1,0:T(8,128)(2,1)S(1)}, u32[]{:S(2)}, u32[]{:S(2)}) collective-permute-start(bf16[256,1024]{1,0:T(8,128)(2,1)S(1)} %get-tuple-element.48), channel_id=1, source_target_pairs={{0,6},{1,7},{2,0},{3,1},{4,2},{5,3},{6,4},{7,5},{8,14},{9,15},{10,... | collective-permute-start | bytes 1572872 | tf_op jit(solution)/shard_map/along_left/ppermute | solution.py:40
  62.1 14.0 %collective-permute-start.19 = (f16[128,1024]{1,0:T(8,128)(2,1)S(1)}, f16[128,1024]{1,0:T(8,128)(2,1)S(1)}, u32[]{:S(2)}, u32[]{:S(2)}) collective-permute-start(f16[128,1024]{1,0:T(8,128)(2,1)S(1)} %get-tuple-element.69), channel_id=1, source_target_pairs={{0,128},{16,144},{32,160},{48,176},{64,192},{80,208},{96,224},{112... | collective-permute-start | bytes 786440 | tf_op jit(solution)/shard_map/island4/ppermute | solution.py:45
  71.2 13.3 %collective-permute-start.20 = (bf16[256,1024]{1,0:T(8,128)(2,1)S(1)}, bf16[256,1024]{1,0:T(8,128)(2,1)S(1)}, u32[]{:S(2)}, u32[]{:S(2)}) collective-permute-start(bf16[256,1024]{1,0:T(8,128)(2,1)S(1)} %get-tuple-element.51.refs_16_), channel_id=1, source_target_pairs={{0,4},{1,5},{2,6},{3,7},{4,0},{5,1},{6,2},{7,3},{8,12},{9,13},{10,... | collective-permute-start | bytes 1572872 | tf_op jit(solution)/shard_map/along_two/ppermute | solution.py:40
  75.5 2.9 %collective-permute-start.17 = (bf16[256,1024]{1,0:T(8,128)(2,1)S(1)}, bf16[256,1024]{1,0:T(8,128)(2,1)S(1)}, u32[]{:S(2)}, u32[]{:S(2)}) collective-permute-start(bf16[256,1024]{1,0:T(8,128)(2,1)S(1)} %get-tuple-element.55), channel_id=1, source_target_pairs={{0,1},{1,0},{2,3},{3,2},{4,5},{5,4},{6,7},{7,6},{8,9},{9,8},{10,11... | collective-permute-start | bytes 1572872 | tf_op jit(solution)/shard_map/got_far/ppermute | solution.py:40
  75.6 2.8 %collective-permute-start.18 = (bf16[256,1024]{1,0:T(8,128)(2,1)S(1)}, bf16[256,1024]{1,0:T(8,128)(2,1)S(1)}, u32[]{:S(2)}, u32[]{:S(2)}) collective-permute-start(bf16[256,1024]{1,0:T(8,128)(2,1)S(1)} %get-tuple-element.56), channel_id=1, source_target_pairs={{0,1},{1,0},{2,3},{3,2},{4,5},{5,4},{6,7},{7,6},{8,9},{9,8},{10,11... | collective-permute-start | bytes 1572872 | tf_op jit(solution)/shard_map/got_terms/ppermute | solution.py:40
  76.4 14.7 %collective-permute-start.21 = (f16[128,1024]{1,0:T(8,128)(2,1)S(1)}, f16[128,1024]{1,0:T(8,128)(2,1)S(1)}, u32[]{:S(2)}, u32[]{:S(2)}) collective-permute-start(f16[128,1024]{1,0:T(8,128)(2,1)S(1)} %get-tuple-element.67), channel_id=1, source_target_pairs={{0,16},{16,0},{32,48},{48,32},{64,80},{80,64},{96,112},{112,96},{1... | collective-permute-start | bytes 786440 | tf_op jit(solution)/shard_map/island5/ppermute | solution.py:45
  (5 other events, 10.3 us)

commit v3 on v2

--- a/solution.py
+++ b/solution.py
@@ -14,7 +14,6 @@
 KV = 1024
 D = 4096
 LIMIT = 14 * 2**20
-NEAR_COST, USE_COST, FAR_COST = 1_000_000, 1_000_000, 8_000_000
 
 RELATIVE = ((1, 1), (1, 3), (1, 2), (1, 0), (0, 1), (0, 3), (0, 2), (0, 0))
 
@@ -67,7 +66,7 @@
         self.scalars = scalars
         self.last = None
 
-    def __call__(self, name, kernel, ins, outs, grid=1, cost=1000):
+    def __call__(self, name, kernel, ins, outs, grid=1):
         arrays, specs, n = [a for a, _ in ins], [spec for _, spec in ins], len(ins)
         tied = self.last is not None
         if tied:
@@ -88,7 +87,7 @@
                 out_specs=[once(spec, grid) for _, _, spec in outs],
             ),
             compiler_params=pltpu.CompilerParams(vmem_limit_bytes=LIMIT),
-            cost_estimate=pl.CostEstimate(flops=0, bytes_accessed=cost, transcendentals=0),
+            cost_estimate=pl.CostEstimate(flops=0, bytes_accessed=1000, transcendentals=0),
         )(self.scalars, *arrays)
         self.last = result[0]
         return result
@@ -97,30 +96,35 @@
         return lax.optimization_barrier((value, self.last))[0]
 
 
-def grad_kernel(s, h, ph, c, pc, *rest):
-    out = rest[-1]
+def grad_kernel(s, h, ph, c, pc, out):
     out[...] = (tdot(h[...], c[...]) + tdot(ph[...], pc[...])).astype(BF)
 
 
-def add_near_kernel(s, h, ph, c, pc, came, _, to_right, to_left):
-    value = (tdot(h[...], c[...]) + tdot(ph[...], pc[...]) + came[...].astype(F32)).astype(BF)
-    for k, out in enumerate((to_right, to_left)):
+def grad_pair_kernel(s, h, ph, c, pc, *outs):
+    value = (tdot(h[...], c[...]) + tdot(ph[...], pc[...])).astype(BF)
+    for k, out in enumerate(outs):
 
         @pl.when(pl.program_id(0) == k)
         def _(out=out):
             out[...] = value
 
 
-def add_far_kernel(s, h, ph, c, pc, came, right, left, out, own):
+def add_near_kernel(s, h, ph, c, pc, came, _, *outs):
+    value = (tdot(h[...], c[...]) + tdot(ph[...], pc[...]) + came[...].astype(F32)).astype(BF)
+    for k, out in enumerate(outs):
+
+        @pl.when(pl.program_id(0) == k)
+        def _(out=out):
+            out[...] = value
+
+
+def add_two_kernel(s, h, ph, c, pc, came, l, r, out):
+    out[...] = (tdot(h[...], c[...]) + tdot(ph[...], pc[...]) + came[...].astype(F32)).astype(BF)
+
+
+def add_own_kernel(s, h, ph, c, pc, came, right, left, out):
     value = tdot(h[...], c[...]) + tdot(ph[...], pc[...]) + came[...].astype(F32)
-
-    @pl.when(pl.program_id(0) == 0)
-    def _():
-        out[...] = value.astype(BF)
-
-    @pl.when(pl.program_id(0) == 1)
-    def _():
-        own[...] = value + right[...].astype(F32) + left[...].astype(F32)
+    out[...] = value + right[...].astype(F32) + left[...].astype(F32)
 
 
 def adam_kernel(s, partial, came, w, m, v, nw, nm, nv):
@@ -240,8 +244,9 @@
 
     (out,) = step("grad_near", grad_kernel, blocks(0), [((2 * B, KV), BF, two)], grid=2)
     y_near = send("half_near", out, half=1)
-    (out,) = step("grad_far", grad_kernel, blocks(2) + [(a, ANY) for a in (w_left, w_right)], [((2 * B, KV), BF, two)], grid=2)
-    y_far = send("half_far", out, half=1)
+    to_two, to_own = step("grad_far", grad_pair_kernel, blocks(2), pair, grid=2)
+    y_two = send("half_two", to_two, half=1)
+    y_own = send("half_own", to_own, half=1)
     w_half = step.after(w_half)
     s2l = send("second_left", w_half, dx=1)
     s2r = send("second_right", w_half, dx=3)
@@ -273,56 +278,62 @@
         return total, trade(name, total, flip)
 
     to_right, to_left = step(
-        "add_near", add_near_kernel, blocks(4) + [(y_near, two), (got0, ANY)], pair, grid=2, cost=NEAR_COST
+        "add_near", add_near_kernel, blocks(4) + [(y_near, two), (got0, ANY)], pair, grid=2
     )
     x1 = send("along_right", to_right, dx=1)
     x3 = send("along_left", to_left, dx=3)
     total, f3 = summed("island3", total, f2, 6)
-    f3, s3l, s3r = lax.optimization_barrier((f3, s3l, s3r))
+
+    (out,) = step(
+        "add_two",
+        add_two_kernel,
+        blocks(6) + [(y_two, at(full)), (s3l, ANY), (s3r, ANY)],
+        [(full, BF, at(full))],
+    )
+    x2 = send("along_two", out, dx=2)
+
     total, f4 = summed("island4", total, f3, 8)
-
-    out, partial = step(
-        "add_far",
-        add_far_kernel,
-        blocks(6) + [(y_far, two), (x1, at(full)), (x3, at(full))],
-        [(full, BF, at(full)), (full, F32, at(full))],
-        grid=2,
-        cost=FAR_COST,
-    )
-    x2 = send("along_two", out, dx=2)
 
     acc, gi1, pgi1, terms = step(
         "far",
         far_kernel,
         chosen(FAR) + [(a, at(full)) for a in (s2l, s2r, s3l, s3r, acc_a, acc_p)],
         [(full, F32, at(full))] + [(full, BF, at(full))] * 3,
-        cost=USE_COST,
     )
     got1 = send("got_far", pgi1, core=1)
     got2 = send("got_terms", terms, core=1)
 
+    (partial,) = step(
+        "add_own",
+        add_own_kernel,
+        blocks(7) + [(a, at(full)) for a in (y_own, x1, x3)],
+        [(full, F32, at(full))],
+    )
+
     total, f5 = summed("island5", total, f4, 1)
 
+    tile = rows(64, lambda k, s: k)
+    new_weight, new_first, new_second = step(
+        "adam",
+        adam_kernel,
+        [(partial, tile), (x2, tile)] + [(a, tile) for a in (w, adam_first[0], adam_second[0])],
+        [(full, BF, tile), (full, F32, tile), (full, F32, tile)],
+        grid=4,
+    )
+    step.last = stay(step.last)
     keys, input_grad = step(
         "finish",
         finish_kernel,
         [(a, at(full)) for a in (acc, gi0, gi1, got0, got1, got2)],
         [(full, BF, at(full)), ((B, D), BF, at((B, D)))],
     )
-    tile = rows(64, lambda k, s: k)
-    new_weight, new_first, new_second = step(
-        "adam",
-        adam_kernel,
-        [(stay(a), tile) for a in (partial, x2, w, adam_first[0], adam_second[0])],
-        [(full, BF, tile), (full, F32, tile), (full, F32, tile)],
-        grid=4,
-    )
+    step.last = stay(step.last)
     half = rows(128, lambda k, s: k)
     new_global, new_momentum = step(
         "merge",
         merge_kernel,
         [(total, rows(128)), (step.after(f5).astype(F32), rows(128))]
-        + [(stay(a), half) for a in (frag_global, frag_momentum)],
+        + [(a, half) for a in (frag_global, frag_momentum)],
         [(full, F32, half)] * 2,
         grid=2,
     )

time: 96.4 us -> 91.9 us (0.953)
  local copies, waits for them, and re-layouts: 4.54 us -> 1.49 us
  Pallas kernels: 32.6 us -> 30.9 us
  waiting for transfers between devices: 19.4 us -> 20.4 us
    unnamed x14 -> x12, local copies, waits for them, and re-layouts: 3.85 us -> 0.8 us
    ppermute x17 -> x18, waiting for transfers between devices: 12.9 us -> 15.6 us  [send(): return lax.ppermute(value, 'fsdp', pairs)]
    ppermute x5, starting transfers between devices: 15.3 us -> 12.9 us  [swap(): return lax.ppermute(value, 'replica', [(r, r ^ flip) for r in range(16)])]
    ppermute x17 -> x18, starting transfers between devices: 20.5 us -> 22.6 us  [send(): return lax.ppermute(value, 'fsdp', pairs)]
    pallas_call x10 -> x11, Pallas kernels: 32.6 us -> 30.9 us  [__call__(): pl.pallas_call(run, name=name, out_shape=[jax.ShapeDtypeStruct(shape, dty...]
    ppermute x5, waiting for transfers between devices: 6.51 us -> 4.8 us  [swap(): return lax.ppermute(value, 'replica', [(r, r ^ flip) for r in range(16)])]
  transfers between devices with their start and end apart: 22 -> 23, of which waited for: 9 -> 7; matrix products, arithmetic and copies ran while one was open for 3% -> 3% of each run, Pallas kernels for 31% -> 32%
where the time goes in v3:
time: 91.9 us; the launch traced here: 91.5 us
  starting transfers between devices  35.5 us (39%)
  Pallas kernels  30.9 us (34%)
  waiting for transfers between devices  20.4 us (22%)
  other arithmetic  2.28 us (2%)
  local copies, waits for them, and re-layouts  1.49 us (2%)
    pallas_call x11, Pallas kernels, __call__(): pl.pallas_call(run, name=name, out_shape=[jax.ShapeDtypeStruct(shape, dty...  30.9 us
    ppermute x18, starting transfers between devices, send(): return lax.ppermute(value, 'fsdp', pairs)  22.6 us
    ppermute x18, waiting for transfers between devices, send(): return lax.ppermute(value, 'fsdp', pairs)  15.6 us
    ppermute x5, starting transfers between devices, swap(): return lax.ppermute(value, 'replica', [(r, r ^ flip) for r in range(16)])  12.9 us
    ppermute x5, waiting for transfers between devices, swap(): return lax.ppermute(value, 'replica', [(r, r ^ flip) for r in range(16)])  4.8 us
    convert_element_type x4, other arithmetic, trade(): return swap(name, value.astype(jnp.float16), flip)  2.24 us
  transfers between devices with their start and end apart: 23, of which 7 were waited for; matrix products, arithmetic and copies ran while one was open for 3% of the time, Pallas kernels for 32%

profile of v3, /device:TPU:6, one launch (start us, length us, event | category | flops | bytes accessed | tf_op | source)
XLA Modules:
  0.0 91.5 jit_solution(14137351063106943404)
XLA Ops:
  1.2 3.2 %collective-permute-start.2 = (bf16[256,1024]{1,0:T(8,128)(2,1)}, bf16[256,1024]{1,0:T(8,128)(2,1)}, u32[]{:S(2)}, u32[]{:S(2)}) collective-permute-start(bf16[256,1024]{1,0:T(8,128)(2,1)} %bitcast.17), channel_id=1, source_target_pairs={{0,8},{1,9},{2,10},{3,11},{4,12},{5,13},{6,14},{7,15},{8,0},{9,1},... | collective-permute-start | bytes 1572872 | tf_op jit(solution)/shard_map/weight_half/ppermute | solution.py:39
  4.4 1.9 %collective-permute-start.7 = (bf16[256,1024]{1,0:T(8,128)(2,1)}, bf16[256,1024]{1,0:T(8,128)(2,1)}, u32[]{:S(2)}, u32[]{:S(2)}) collective-permute-start(bf16[256,1024]{1,0:T(8,128)(2,1)} %bitcast.48), channel_id=1, source_target_pairs={{0,16},{16,0},{32,48},{48,32},{64,80},{80,64},{96,112},{112,96},{1... | collective-permute-start | bytes 1572872 | tf_op jit(solution)/shard_map/island1/ppermute | solution.py:44
  7.2 2.4 %collective-permute-start.5 = (bf16[256,1024]{1,0:T(8,128)(2,1)}, bf16[256,1024]{1,0:T(8,128)(2,1)}, u32[]{:S(2)}, u32[]{:S(2)}) collective-permute-start(bf16[256,1024]{1,0:T(8,128)(2,1)} %bitcast.19), channel_id=1, source_target_pairs={{0,2},{1,3},{2,4},{3,5},{4,6},{5,7},{6,0},{7,1},{8,10},{9,11},{10,... | collective-permute-start | bytes 1572872 | tf_op jit(solution)/shard_map/weight_left/ppermute | solution.py:39
  10.3 3.4 %grad_near.1.refs_4_ = bf16[512,1024]{1,0:T(8,128)(2,1)} custom-call(s32[16]{0:T(128)S(1)} %fusion.3.s, bf16[256,4096]{1,0:T(8,128)(2,1)} %bitcast.25, bf16[256,4096]{1,0:T(8,128)(2,1)S(1)} %collective-permute-done.refs_1_.refs_4_.refs_5_.refs_6_.refs_7_, bf16[256,1024]{1,0:T(8,128)(2,1)} %bitcast.39, ...), custom_call_target="tpu_custom_call" | custom-call | bytes 1000 | tf_op jit(solution)/shard_map/grad_near/pallas_call | solution.py:79
  14.1 2.7 %grad_far.1 = (bf16[256,1024]{1,0:T(8,128)(2,1)S(1)}, bf16[256,1024]{1,0:T(8,128)(2,1)S(1)}) custom-call(s32[16]{0:T(128)S(1)} %fusion.3.s, bf16[256,4096]{1,0:T(8,128)(2,1)} %bitcast.26, bf16[256,4096]{1,0:T(8,128)(2,1)S(1)} %collective-permute-done.refs_1_.refs_4_.refs_5_.refs_6_.refs_7_, bf16[256,1024]{1,0:T(8,128)(2,1)} %bitcast.40, ...), custom_call_target="tpu_custom_call" | custom-call | bytes 1000 | tf_op jit(solution)/shard_map/grad_far/pallas_call | solution.py:79
  21.9 4.5 %near.1 = (f32[256,1024]{1,0:T(8,128)S(1)}, f32[256,1024]{1,0:T(8,128)S(1)}, bf16[256,1024]{1,0:T(8,128)(2,1)S(1)}, bf16[256,1024]{1,0:T(8,128)(2,1)S(1)}) custom-call(s32[16]{0:T(128)S(1)} %fusion.3.s, bf16[256,4096]{1,0:T(8,128)(2,1)} %bitcast.27, bf16[256,4096]{1,0:T(8,128)(2,1)} %bitcast.28, bf16[256,4096]{1,0:T(8,128)(2,1)} %bitcast.29, ...), custom_call_target="tpu_custom_call" | custom-call | bytes 1000 | tf_op jit(solution)/shard_map/near/pallas_call | solution.py:79
  26.6 3.3 %collective-permute-start.10 = (f16[128,1024]{1,0:T(8,128)(2,1)S(1)}, f16[128,1024]{1,0:T(8,128)(2,1)S(1)}, u32[]{:S(2)}, u32[]{:S(2)}) collective-permute-start(f16[128,1024]{1,0:T(8,128)(2,1)S(1)} %get-tuple-element.67), channel_id=1, source_target_pairs={{0,32},{16,48},{32,0},{48,16},{64,96},{80,112},{96,64},{112,80},{1... | collective-permute-start | bytes 786440 | tf_op jit(solution)/shard_map/island2/ppermute | solution.py:44
  29.9 2.4 %collective-permute-done.4.refs_3_.refs_11_ = bf16[256,1024]{1,0:T(8,128)(2,1)S(1)} collective-permute-done((bf16[256,1024]{1,0:T(8,128)(2,1)}, bf16[256,1024]{1,0:T(8,128)(2,1)S(1)}, u32[]{:S(2)}, u32[]{:S(2)}) %collective-permute-start.4) | collective-permute-done | bytes 524320 | tf_op jit(solution)/shard_map/second_right/ppermute | solution.py:39
  32.4 2.3 %collective-permute-start.14 = (bf16[256,1024]{1,0:T(8,128)(2,1)S(1)}, bf16[256,1024]{1,0:T(8,128)(2,1)S(1)}, u32[]{:S(2)}, u32[]{:S(2)}) collective-permute-start(bf16[256,1024]{1,0:T(8,128)(2,1)S(1)} %get-tuple-element.34), channel_id=1, source_target_pairs={{0,8},{1,9},{2,10},{3,11},{4,12},{5,13},{6,14},{7,15},{8,0},{9,1},... | collective-permute-start | bytes 1572872 | tf_op jit(solution)/shard_map/half_two/ppermute | solution.py:39
  36.4 3.2 %collective-permute-start.8 = (bf16[256,1024]{1,0:T(8,128)(2,1)S(1)}, bf16[256,1024]{1,0:T(8,128)(2,1)S(1)}, u32[]{:S(2)}, u32[]{:S(2)}) collective-permute-start(bf16[256,1024]{1,0:T(8,128)(2,1)S(1)} %get-tuple-element.38.refs_6_), channel_id=1, source_target_pairs={{0,2},{1,3},{2,4},{3,5},{4,6},{5,7},{6,0},{7,1},{8,10},{9,11},{10,... | collective-permute-start | bytes 1572872 | tf_op jit(solution)/shard_map/third_left/ppermute | solution.py:39
  39.6 2.1 %collective-permute-done.11.refs_4_ = bf16[512,1024]{1,0:T(8,128)(2,1)} collective-permute-done((bf16[512,1024]{1,0:T(8,128)(2,1)}, bf16[512,1024]{1,0:T(8,128)(2,1)}, u32[]{:S(2)}, u32[]{:S(2)}) %collective-permute-start.11) | collective-permute-done | bytes 1048608 | tf_op jit(solution)/shard_map/half_near/ppermute | solution.py:39
  41.6 2.9 %add_near.1 = (bf16[256,1024]{1,0:T(8,128)(2,1)S(1)}, bf16[256,1024]{1,0:T(8,128)(2,1)S(1)}) custom-call(s32[16]{0:T(128)S(1)} %fusion.3.s, bf16[256,4096]{1,0:T(8,128)(2,1)} %bitcast.31, bf16[256,4096]{1,0:T(8,128)(2,1)S(1)} %collective-permute-done.refs_1_.refs_4_.refs_5_.refs_6_.refs_7_, bf16[256,1024]{1,0:T(8,128)(2,1)} %bitcast.42, ...), custom_call_target="tpu_custom_call" | custom-call | bytes 1000 | tf_op jit(solution)/shard_map/add_near/pallas_call | solution.py:79
  44.9 5.5 %collective-permute-start.13 = (f16[128,1024]{1,0:T(8,128)(2,1)S(1)}, f16[128,1024]{1,0:T(8,128)(2,1)S(1)}, u32[]{:S(2)}, u32[]{:S(2)}) collective-permute-start(f16[128,1024]{1,0:T(8,128)(2,1)S(1)} %get-tuple-element.65), channel_id=1, source_target_pairs={{0,96},{16,112},{32,64},{48,80},{64,32},{80,48},{96,0},{112,16},{1... | collective-permute-start | bytes 786440 | tf_op jit(solution)/shard_map/island3/ppermute | solution.py:44
  50.4 2.8 %collective-permute-start.17 = (bf16[256,1024]{1,0:T(8,128)(2,1)S(1)}, bf16[256,1024]{1,0:T(8,128)(2,1)S(1)}, u32[]{:S(2)}, u32[]{:S(2)}) collective-permute-start(bf16[256,1024]{1,0:T(8,128)(2,1)S(1)} %get-tuple-element.50), channel_id=1, source_target_pairs={{0,8},{1,9},{2,10},{3,11},{4,12},{5,13},{6,14},{7,15},{8,0},{9,1},... | collective-permute-start | bytes 1572872 | tf_op jit(solution)/shard_map/half_own/ppermute | solution.py:39
  55.2 2.1 %add_two.1 = bf16[256,1024]{1,0:T(8,128)(2,1)S(1)} custom-call(s32[16]{0:T(128)S(1)} %fusion.3.s, bf16[256,4096]{1,0:T(8,128)(2,1)} %bitcast.32, bf16[256,4096]{1,0:T(8,128)(2,1)S(1)} %collective-permute-done.refs_1_.refs_4_.refs_5_.refs_6_.refs_7_, bf16[256,1024]{1,0:T(8,128)(2,1)} %bitcast.43, ...), custom_call_target="tpu_custom_call" | custom-call | bytes 1000 | tf_op jit(solution)/shard_map/add_two/pallas_call | solution.py:79
  57.3 2.0 %collective-permute-done.13 = f16[128,1024]{1,0:T(8,128)(2,1)S(1)} collective-permute-done((f16[128,1024]{1,0:T(8,128)(2,1)S(1)}, f16[128,1024]{1,0:T(8,128)(2,1)S(1)}, u32[]{:S(2)}, u32[]{:S(2)}) %collective-permute-start.13) | collective-permute-done | bytes 262176 | tf_op jit(solution)/shard_map/island3/ppermute | solution.py:44
  59.6 2.1 %collective-permute-start.21 = (f16[128,1024]{1,0:T(8,128)(2,1)S(1)}, f16[128,1024]{1,0:T(8,128)(2,1)S(1)}, u32[]{:S(2)}, u32[]{:S(2)}) collective-permute-start(f16[128,1024]{1,0:T(8,128)(2,1)S(1)} %get-tuple-element.63), channel_id=1, source_target_pairs={{0,128},{16,144},{32,160},{48,176},{64,192},{80,208},{96,224},{112... | collective-permute-start | bytes 786440 | tf_op jit(solution)/shard_map/island4/ppermute | solution.py:44
  63.1 4.3 %far.1 = (f32[256,1024]{1,0:T(8,128)S(1)}, bf16[256,1024]{1,0:T(8,128)(2,1)S(1)}, bf16[256,1024]{1,0:T(8,128)(2,1)S(1)}, bf16[256,1024]{1,0:T(8,128)(2,1)S(1)}) custom-call(s32[16]{0:T(128)S(1)} %fusion.3.s, bf16[256,4096]{1,0:T(8,128)(2,1)} %bitcast.33, bf16[256,4096]{1,0:T(8,128)(2,1)} %bitcast.34, bf16[256,4096]{1,0:T(8,128)(2,1)} %bitcast.35, ...), custom_call_target="tpu_custom_call" | custom-call | bytes 1000 | tf_op jit(solution)/shard_map/far/pallas_call | solution.py:79
  67.5 10.6 %collective-permute-done.19.refs_6_ = bf16[256,1024]{1,0:T(8,128)(2,1)S(1)} collective-permute-done((bf16[256,1024]{1,0:T(8,128)(2,1)S(1)}, bf16[256,1024]{1,0:T(8,128)(2,1)S(1)}, u32[]{:S(2)}, u32[]{:S(2)}) %collective-permute-start.19) | collective-permute-done | bytes 524320 | tf_op jit(solution)/shard_map/along_left/ppermute | solution.py:39
  78.1 2.2 %add_own.1.refs_0_ = f32[256,1024]{1,0:T(8,128)S(1)} custom-call(s32[16]{0:T(128)S(1)} %fusion.3.s, bf16[256,4096]{1,0:T(8,128)(2,1)} %bitcast.37, bf16[256,4096]{1,0:T(8,128)(2,1)S(1)} %collective-permute-done.refs_1_.refs_4_.refs_5_.refs_6_.refs_7_, bf16[256,1024]{1,0:T(8,128)(2,1)} %bitcast.45, ...), custom_call_target="tpu_custom_call" | custom-call | bytes 1000 | tf_op jit(solution)/shard_map/add_own/pallas_call | solution.py:79
  81.5 2.7 %adam.1 = (bf16[256,1024]{1,0:T(8,128)(2,1)}, f32[256,1024]{1,0:T(8,128)}, f32[256,1024]{1,0:T(8,128)}) custom-call(s32[16]{0:T(128)S(1)} %fusion.3.s, f32[256,1024]{1,0:T(8,128)S(1)} %add_own.1.refs_0_, bf16[256,1024]{1,0:T(8,128)(2,1)S(1)} %collective-permute-done.20.refs_1_, bf16[256,1024]{1,0:T(8,128)(2,1)S(1)} %bitcast.21, f32[256,1024]{1,0:T(8,128)S(1)} %bitcast.22, ...), custom_call_target="tpu_custom_call" | custom-call | bytes 1000 | tf_op jit(solution)/shard_map/adam/pallas_call | solution.py:79
  84.2 2.4 %finish.1 = (bf16[256,1024]{1,0:T(8,128)(2,1)}, bf16[256,4096]{1,0:T(8,128)(2,1)}) custom-call(s32[16]{0:T(128)S(1)} %fusion.3.s, f32[256,1024]{1,0:T(8,128)S(1)} %get-tuple-element.45.refs_7_.refs_0_, bf16[256,1024]{1,0:T(8,128)(2,1)S(1)} %get-tuple-element.46.refs_1_, bf16[256,1024]{1,0:T(8,128)(2,1)S(1)} %get-tuple-element.47.refs_2_, ...), custom_call_target="tpu_custom_call" | custom-call | bytes 1000 | tf_op jit(solution)/shard_map/finish/pallas_call | solution.py:79
  86.6 2.8 %collective-permute-done.22 = f16[128,1024]{1,0:T(8,128)(2,1)S(1)} collective-permute-done((f16[128,1024]{1,0:T(8,128)(2,1)S(1)}, f16[128,1024]{1,0:T(8,128)(2,1)S(1)}, u32[]{:S(2)}, u32[]{:S(2)}) %collective-permute-start.22) | collective-permute-done | bytes 262176 | tf_op jit(solution)/shard_map/island5/ppermute | solution.py:44
  89.5 2.0 %merge.1 = (f32[256,1024]{1,0:T(8,128)}, f32[256,1024]{1,0:T(8,128)}) custom-call(s32[16]{0:T(128)S(1)} %fusion.3.s, f32[128,1024]{1,0:T(8,128)S(1)} %get-tuple-element.62.refs_5_.refs_0_, f32[128,1024]{1,0:T(8,128)S(1)} %convert_element_type.43.refs_1_, f32[256,1024]{1,0:T(8,128)S(1)} %copy-done, f32[256,1024]{1,0:T(8,128)S(1)} %copy-done.4, ...), custom_call_target="tpu_custom_call" | custom-call | bytes 1000 | tf_op jit(solution)/shard_map/merge/pallas_call | solution.py:79
  (51 shorter events, 14.7 us)
Async XLA Ops:
  0.6 9.6 %collective-permute-start = (bf16[256,4096]{1,0:T(8,128)(2,1)}, bf16[256,4096]{1,0:T(8,128)(2,1)S(1)}, u32[]{:S(2)}, u32[]{:S(2)}) collective-permute-start(bf16[256,4096]{1,0:T(8,128)(2,1)} %bitcast.24), channel_id=1, source_target_pairs={{0,1},{1,0},{2,3},{3,2},{4,5},{5,4},{6,7},{7,6},{8,9},{9,8},{10,11... | collective-permute-start | bytes 6291464 | tf_op jit(solution)/shard_map/peer_hidden/ppermute | solution.py:39
  0.7 6.4 %collective-permute-start.1 = (bf16[256,1024]{1,0:T(8,128)(2,1)}, bf16[256,1024]{1,0:T(8,128)(2,1)S(1)}, u32[]{:S(2)}, u32[]{:S(2)}) collective-permute-start(bf16[256,1024]{1,0:T(8,128)(2,1)} %bitcast.38), channel_id=1, source_target_pairs={{0,1},{1,0},{2,3},{3,2},{4,5},{5,4},{6,7},{7,6},{8,9},{9,8},{10,11... | collective-permute-start | bytes 1572872 | tf_op jit(solution)/shard_map/peer_cotangent/ppermute | solution.py:39
  1.2 15.8 %collective-permute-start.2 = (bf16[256,1024]{1,0:T(8,128)(2,1)}, bf16[256,1024]{1,0:T(8,128)(2,1)}, u32[]{:S(2)}, u32[]{:S(2)}) collective-permute-start(bf16[256,1024]{1,0:T(8,128)(2,1)} %bitcast.17), channel_id=1, source_target_pairs={{0,8},{1,9},{2,10},{3,11},{4,12},{5,13},{6,14},{7,15},{8,0},{9,1},... | collective-permute-start | bytes 1572872 | tf_op jit(solution)/shard_map/weight_half/ppermute | solution.py:39
  4.4 14.2 %collective-permute-start.7 = (bf16[256,1024]{1,0:T(8,128)(2,1)}, bf16[256,1024]{1,0:T(8,128)(2,1)}, u32[]{:S(2)}, u32[]{:S(2)}) collective-permute-start(bf16[256,1024]{1,0:T(8,128)(2,1)} %bitcast.48), channel_id=1, source_target_pairs={{0,16},{16,0},{32,48},{48,32},{64,80},{80,64},{96,112},{112,96},{1... | collective-permute-start | bytes 1572872 | tf_op jit(solution)/shard_map/island1/ppermute | solution.py:44
  6.3 15.6 %collective-permute-start.6 = (bf16[256,1024]{1,0:T(8,128)(2,1)}, bf16[256,1024]{1,0:T(8,128)(2,1)S(1)}, u32[]{:S(2)}, u32[]{:S(2)}) collective-permute-start(bf16[256,1024]{1,0:T(8,128)(2,1)} %bitcast.18), channel_id=1, source_target_pairs={{0,6},{1,7},{2,0},{3,1},{4,2},{5,3},{6,4},{7,5},{8,14},{9,15},{10,... | collective-permute-start | bytes 1572872 | tf_op jit(solution)/shard_map/weight_right/ppermute | solution.py:39
  7.2 14.8 %collective-permute-start.5 = (bf16[256,1024]{1,0:T(8,128)(2,1)}, bf16[256,1024]{1,0:T(8,128)(2,1)}, u32[]{:S(2)}, u32[]{:S(2)}) collective-permute-start(bf16[256,1024]{1,0:T(8,128)(2,1)} %bitcast.19), channel_id=1, source_target_pairs={{0,2},{1,3},{2,4},{3,5},{4,6},{5,7},{6,0},{7,1},{8,10},{9,11},{10,... | collective-permute-start | bytes 1572872 | tf_op jit(solution)/shard_map/weight_left/ppermute | solution.py:39
  13.7 27.9 %collective-permute-start.11 = (bf16[512,1024]{1,0:T(8,128)(2,1)}, bf16[512,1024]{1,0:T(8,128)(2,1)}, u32[]{:S(2)}, u32[]{:S(2)}) collective-permute-start(bf16[512,1024]{1,0:T(8,128)(2,1)} %grad_near.1.refs_4_), channel_id=1, source_target_pairs={{0,8},{1,9},{2,10},{3,11},{4,12},{5,13},{6,14},{7,15},{8,0},{9,1},... | collective-permute-start | bytes 3145736 | tf_op jit(solution)/shard_map/half_near/ppermute | solution.py:39
  14.0 6.2 %copy-start.5 = (bf16[1,256,1024]{2,1,0:T(8,128)(2,1)S(1)}, bf16[1,256,1024]{2,1,0:T(8,128)(2,1)}, u32[]{:S(2)}) copy-start(bf16[1,256,1024]{2,1,0:T(8,128)(2,1)} %param.16) | copy-start | bytes 1572868
  17.0 15.3 %collective-permute-start.4 = (bf16[256,1024]{1,0:T(8,128)(2,1)}, bf16[256,1024]{1,0:T(8,128)(2,1)S(1)}, u32[]{:S(2)}, u32[]{:S(2)}) collective-permute-start(bf16[256,1024]{1,0:T(8,128)(2,1)} %collective-permute-done.2.refs_11_), channel_id=1, source_target_pairs={{0,6},{1,7},{2,0},{3,1},{4,2},{5,3},{6,4},{7,5},{8,14},{9,15},{10,... | collective-permute-start | bytes 1572872 | tf_op jit(solution)/shard_map/second_right/ppermute | solution.py:39
  18.7 16.0 %collective-permute-start.3 = (bf16[256,1024]{1,0:T(8,128)(2,1)}, bf16[256,1024]{1,0:T(8,128)(2,1)S(1)}, u32[]{:S(2)}, u32[]{:S(2)}) collective-permute-start(bf16[256,1024]{1,0:T(8,128)(2,1)} %collective-permute-done.2.refs_11_), channel_id=1, source_target_pairs={{0,2},{1,3},{2,4},{3,5},{4,6},{5,7},{6,0},{7,1},{8,10},{9,11},{10,... | collective-permute-start | bytes 1572872 | tf_op jit(solution)/shard_map/second_left/ppermute | solution.py:39
  26.5 9.9 %collective-permute-start.12 = (bf16[256,1024]{1,0:T(8,128)(2,1)S(1)}, bf16[256,1024]{1,0:T(8,128)(2,1)S(1)}, u32[]{:S(2)}, u32[]{:S(2)}) collective-permute-start(bf16[256,1024]{1,0:T(8,128)(2,1)S(1)} %get-tuple-element.41), channel_id=1, source_target_pairs={{0,1},{1,0},{2,3},{3,2},{4,5},{5,4},{6,7},{7,6},{8,9},{9,8},{10,11... | collective-permute-start | bytes 1572872 | tf_op jit(solution)/shard_map/got_near/ppermute | solution.py:39
  26.6 18.0 %collective-permute-start.10 = (f16[128,1024]{1,0:T(8,128)(2,1)S(1)}, f16[128,1024]{1,0:T(8,128)(2,1)S(1)}, u32[]{:S(2)}, u32[]{:S(2)}) collective-permute-start(f16[128,1024]{1,0:T(8,128)(2,1)S(1)} %get-tuple-element.67), channel_id=1, source_target_pairs={{0,32},{16,48},{32,0},{48,16},{64,96},{80,112},{96,64},{112,80},{1... | collective-permute-start | bytes 786440 | tf_op jit(solution)/shard_map/island2/ppermute | solution.py:44
  32.4 20.8 %collective-permute-start.14 = (bf16[256,1024]{1,0:T(8,128)(2,1)S(1)}, bf16[256,1024]{1,0:T(8,128)(2,1)S(1)}, u32[]{:S(2)}, u32[]{:S(2)}) collective-permute-start(bf16[256,1024]{1,0:T(8,128)(2,1)S(1)} %get-tuple-element.34), channel_id=1, source_target_pairs={{0,8},{1,9},{2,10},{3,11},{4,12},{5,13},{6,14},{7,15},{8,0},{9,1},... | collective-permute-start | bytes 1572872 | tf_op jit(solution)/shard_map/half_two/ppermute | solution.py:39
  36.3 17.4 %collective-permute-start.9 = (bf16[256,1024]{1,0:T(8,128)(2,1)S(1)}, bf16[256,1024]{1,0:T(8,128)(2,1)S(1)}, u32[]{:S(2)}, u32[]{:S(2)}) collective-permute-start(bf16[256,1024]{1,0:T(8,128)(2,1)S(1)} %get-tuple-element.39), channel_id=1, source_target_pairs={{0,6},{1,7},{2,0},{3,1},{4,2},{5,3},{6,4},{7,5},{8,14},{9,15},{10,... | collective-permute-start | bytes 1572872 | tf_op jit(solution)/shard_map/third_right/ppermute | solution.py:39
  36.4 18.8 %collective-permute-start.8 = (bf16[256,1024]{1,0:T(8,128)(2,1)S(1)}, bf16[256,1024]{1,0:T(8,128)(2,1)S(1)}, u32[]{:S(2)}, u32[]{:S(2)}) collective-permute-start(bf16[256,1024]{1,0:T(8,128)(2,1)S(1)} %get-tuple-element.38.refs_6_), channel_id=1, source_target_pairs={{0,2},{1,3},{2,4},{3,5},{4,6},{5,7},{6,0},{7,1},{8,10},{9,11},{10,... | collective-permute-start | bytes 1572872 | tf_op jit(solution)/shard_map/third_left/ppermute | solution.py:39
  44.9 14.4 %collective-permute-start.13 = (f16[128,1024]{1,0:T(8,128)(2,1)S(1)}, f16[128,1024]{1,0:T(8,128)(2,1)S(1)}, u32[]{:S(2)}, u32[]{:S(2)}) collective-permute-start(f16[128,1024]{1,0:T(8,128)(2,1)S(1)} %get-tuple-element.65), channel_id=1, source_target_pairs={{0,96},{16,112},{32,64},{48,80},{64,32},{80,48},{96,0},{112,16},{1... | collective-permute-start | bytes 786440 | tf_op jit(solution)/shard_map/island3/ppermute | solution.py:44
  50.4 17.0 %collective-permute-start.17 = (bf16[256,1024]{1,0:T(8,128)(2,1)S(1)}, bf16[256,1024]{1,0:T(8,128)(2,1)S(1)}, u32[]{:S(2)}, u32[]{:S(2)}) collective-permute-start(bf16[256,1024]{1,0:T(8,128)(2,1)S(1)} %get-tuple-element.50), channel_id=1, source_target_pairs={{0,8},{1,9},{2,10},{3,11},{4,12},{5,13},{6,14},{7,15},{8,0},{9,1},... | collective-permute-start | bytes 1572872 | tf_op jit(solution)/shard_map/half_own/ppermute | solution.py:39
  53.1 24.9 %collective-permute-start.18 = (bf16[256,1024]{1,0:T(8,128)(2,1)S(1)}, bf16[256,1024]{1,0:T(8,128)(2,1)S(1)}, u32[]{:S(2)}, u32[]{:S(2)}) collective-permute-start(bf16[256,1024]{1,0:T(8,128)(2,1)S(1)} %get-tuple-element.42), channel_id=1, source_target_pairs={{0,2},{1,3},{2,4},{3,5},{4,6},{5,7},{6,0},{7,1},{8,10},{9,11},{10,... | collective-permute-start | bytes 1572872 | tf_op jit(solution)/shard_map/along_right/ppermute | solution.py:39
  53.6 24.4 %collective-permute-start.19 = (bf16[256,1024]{1,0:T(8,128)(2,1)S(1)}, bf16[256,1024]{1,0:T(8,128)(2,1)S(1)}, u32[]{:S(2)}, u32[]{:S(2)}) collective-permute-start(bf16[256,1024]{1,0:T(8,128)(2,1)S(1)} %get-tuple-element.51), channel_id=1, source_target_pairs={{0,6},{1,7},{2,0},{3,1},{4,2},{5,3},{6,4},{7,5},{8,14},{9,15},{10,... | collective-permute-start | bytes 1572872 | tf_op jit(solution)/shard_map/along_left/ppermute | solution.py:39
  59.6 20.7 %collective-permute-start.21 = (f16[128,1024]{1,0:T(8,128)(2,1)S(1)}, f16[128,1024]{1,0:T(8,128)(2,1)S(1)}, u32[]{:S(2)}, u32[]{:S(2)}) collective-permute-start(f16[128,1024]{1,0:T(8,128)(2,1)S(1)} %get-tuple-element.63), channel_id=1, source_target_pairs={{0,128},{16,144},{32,160},{48,176},{64,192},{80,208},{96,224},{112... | collective-permute-start | bytes 786440 | tf_op jit(solution)/shard_map/island4/ppermute | solution.py:44
  61.7 19.0 %collective-permute-start.20 = (bf16[256,1024]{1,0:T(8,128)(2,1)S(1)}, bf16[256,1024]{1,0:T(8,128)(2,1)S(1)}, u32[]{:S(2)}, u32[]{:S(2)}) collective-permute-start(bf16[256,1024]{1,0:T(8,128)(2,1)S(1)} %add_two.1), channel_id=1, source_target_pairs={{0,4},{1,5},{2,6},{3,7},{4,0},{5,1},{6,2},{7,3},{8,12},{9,13},{10,... | collective-permute-start | bytes 1572872 | tf_op jit(solution)/shard_map/along_two/ppermute | solution.py:39
  67.4 16.8 %collective-permute-start.15 = (bf16[256,1024]{1,0:T(8,128)(2,1)S(1)}, bf16[256,1024]{1,0:T(8,128)(2,1)S(1)}, u32[]{:S(2)}, u32[]{:S(2)}) collective-permute-start(bf16[256,1024]{1,0:T(8,128)(2,1)S(1)} %get-tuple-element.48), channel_id=1, source_target_pairs={{0,1},{1,0},{2,3},{3,2},{4,5},{5,4},{6,7},{7,6},{8,9},{9,8},{10,11... | collective-permute-start | bytes 1572872 | tf_op jit(solution)/shard_map/got_far/ppermute | solution.py:39
  78.1 6.2 %collective-permute-start.16 = (bf16[256,1024]{1,0:T(8,128)(2,1)S(1)}, bf16[256,1024]{1,0:T(8,128)(2,1)S(1)}, u32[]{:S(2)}, u32[]{:S(2)}) collective-permute-start(bf16[256,1024]{1,0:T(8,128)(2,1)S(1)} %get-tuple-element.49), channel_id=1, source_target_pairs={{0,1},{1,0},{2,3},{3,2},{4,5},{5,4},{6,7},{7,6},{8,9},{9,8},{10,11... | collective-permute-start | bytes 1572872 | tf_op jit(solution)/shard_map/got_terms/ppermute | solution.py:39
  80.6 8.8 %collective-permute-start.22 = (f16[128,1024]{1,0:T(8,128)(2,1)S(1)}, f16[128,1024]{1,0:T(8,128)(2,1)S(1)}, u32[]{:S(2)}, u32[]{:S(2)}) collective-permute-start(f16[128,1024]{1,0:T(8,128)(2,1)S(1)} %get-tuple-element.61), channel_id=1, source_target_pairs={{0,16},{16,0},{32,48},{48,32},{64,80},{80,64},{96,112},{112,96},{1... | collective-permute-start | bytes 786440 | tf_op jit(solution)/shard_map/island5/ppermute | solution.py:44
  (5 other events, 20.5 us)

commit v4 on v3

--- a/solution.py
+++ b/solution.py
@@ -96,10 +96,6 @@
         return lax.optimization_barrier((value, self.last))[0]
 
 
-def grad_kernel(s, h, ph, c, pc, out):
-    out[...] = (tdot(h[...], c[...]) + tdot(ph[...], pc[...])).astype(BF)
-
-
 def grad_pair_kernel(s, h, ph, c, pc, *outs):
     value = (tdot(h[...], c[...]) + tdot(ph[...], pc[...])).astype(BF)
     for k, out in enumerate(outs):
@@ -109,17 +105,8 @@
             out[...] = value
 
 
-def add_near_kernel(s, h, ph, c, pc, came, _, *outs):
-    value = (tdot(h[...], c[...]) + tdot(ph[...], pc[...]) + came[...].astype(F32)).astype(BF)
-    for k, out in enumerate(outs):
-
-        @pl.when(pl.program_id(0) == k)
-        def _(out=out):
-            out[...] = value
-
-
-def add_two_kernel(s, h, ph, c, pc, came, l, r, out):
-    out[...] = (tdot(h[...], c[...]) + tdot(ph[...], pc[...]) + came[...].astype(F32)).astype(BF)
+def add_kernel(s, h, ph, c, pc, came, *refs):
+    refs[-1][...] = (tdot(h[...], c[...]) + tdot(ph[...], pc[...]) + came[...].astype(F32)).astype(BF)
 
 
 def add_own_kernel(s, h, ph, c, pc, came, right, left, out):
@@ -239,11 +226,11 @@
         picks = [at((B, B), 0, lambda _, s, k=k: s[k]) for k in order]
         return [(h, p) for p in picks] + [(ph, p) for p in picks] + [(c, at(full)), (pc, at(full))]
 
-    two = rows(B, lambda k, s: k)
     pair = [(full, BF, at(full))] * 2
 
-    (out,) = step("grad_near", grad_kernel, blocks(0), [((2 * B, KV), BF, two)], grid=2)
-    y_near = send("half_near", out, half=1)
+    to_right, to_left = step("grad_near", grad_pair_kernel, blocks(0), pair, grid=2)
+    y_right = send("half_right", to_right, half=1)
+    y_left = send("half_left", to_left, half=1)
     to_two, to_own = step("grad_far", grad_pair_kernel, blocks(2), pair, grid=2)
     y_two = send("half_two", to_two, half=1)
     y_own = send("half_own", to_own, half=1)
@@ -264,6 +251,9 @@
         [(full, F32, at(full))] * 2 + [(full, BF, at(full))] * 2,
     )
     got0 = send("got_near", pgi0, core=1)
+    (out,) = step("add_right", add_kernel, blocks(4) + [(y_right, at(full))], [(full, BF, at(full))])
+    x1 = send("along_right", out, dx=1)
+
     to_right, to_left = step(
         "forward",
         forward_kernel,
@@ -277,17 +267,15 @@
         step.last = total = rounded(total + step.after(came).astype(F32))
         return total, trade(name, total, flip)
 
-    to_right, to_left = step(
-        "add_near", add_near_kernel, blocks(4) + [(y_near, two), (got0, ANY)], pair, grid=2
-    )
-    x1 = send("along_right", to_right, dx=1)
-    x3 = send("along_left", to_left, dx=3)
+    (out,) = step("add_left", add_kernel, blocks(5) + [(y_left, at(full)), (got0, ANY)], [(full, BF, at(full))])
+    x3 = send("along_left", out, dx=3)
+
     total, f3 = summed("island3", total, f2, 6)
 
     (out,) = step(
         "add_two",
-        add_two_kernel,
-        blocks(6) + [(y_two, at(full)), (s3l, ANY), (s3r, ANY)],
+        add_kernel,
+        blocks(6) + [(y_two, at(full)), (s3l, ANY), (s3r, ANY), (x1, ANY)],
         [(full, BF, at(full))],
     )
     x2 = send("along_two", out, dx=2)

time: 91.9 us -> 91.2 us (level)
  waiting for transfers between devices: 20.4 us -> 16.7 us
  Pallas kernels: 30.9 us -> 32.5 us
  starting transfers between devices: 35.5 us -> 37 us
    ppermute x5, waiting for transfers between devices: 4.8 us -> 0.48 us  [swap(): return lax.ppermute(value, 'replica', [(r, r ^ flip) for r in range(16)])]
    ppermute x5, starting transfers between devices: 12.9 us -> 14.6 us  [swap(): return lax.ppermute(value, 'replica', [(r, r ^ flip) for r in range(16)])]
    pallas_call x11 -> x12, Pallas kernels: 30.9 us -> 32.5 us  [__call__(): pl.pallas_call(run, name=name, out_shape=[jax.ShapeDtypeStruct(shape, dty...]
    ppermute x18 -> x19, waiting for transfers between devices: 15.6 us -> 16.2 us  [send(): return lax.ppermute(value, 'fsdp', pairs)]
    ppermute x18 -> x19, starting transfers between devices: 22.6 us -> 22.5 us  [send(): return lax.ppermute(value, 'fsdp', pairs)]
  transfers between devices with their start and end apart: 23 -> 24, of which waited for: 7 -> 5; matrix products, arithmetic and copies ran while one was open for 3% -> 3% of each run, Pallas kernels for 32% -> 34%
where the time goes in v4:
time: 91.2 us; the launch traced here: 90.8 us
  starting transfers between devices  37 us (41%)
  Pallas kernels  32.5 us (36%)
  waiting for transfers between devices  16.7 us (18%)
  other arithmetic  2.28 us (2%)
  local copies, waits for them, and re-layouts  1.52 us (2%)
    pallas_call x12, Pallas kernels, __call__(): pl.pallas_call(run, name=name, out_shape=[jax.ShapeDtypeStruct(shape, dty...  32.5 us
    ppermute x19, starting transfers between devices, send(): return lax.ppermute(value, 'fsdp', pairs)  22.5 us
    ppermute x19, waiting for transfers between devices, send(): return lax.ppermute(value, 'fsdp', pairs)  16.2 us
    ppermute x5, starting transfers between devices, swap(): return lax.ppermute(value, 'replica', [(r, r ^ flip) for r in range(16)])  14.6 us
    convert_element_type x4, other arithmetic, trade(): return swap(name, value.astype(jnp.float16), flip)  2.24 us
  transfers between devices with their start and end apart: 24, of which 5 were waited for; matrix products, arithmetic and copies ran while one was open for 3% of the time, Pallas kernels for 34%

profile of v4, /device:TPU:6, one launch (start us, length us, event | category | flops | bytes accessed | tf_op | source)
XLA Modules:
  0.0 90.8 jit_solution(10589381308966567346)
XLA Ops:
  1.2 3.2 %collective-permute-start.2 = (bf16[256,1024]{1,0:T(8,128)(2,1)}, bf16[256,1024]{1,0:T(8,128)(2,1)}, u32[]{:S(2)}, u32[]{:S(2)}) collective-permute-start(bf16[256,1024]{1,0:T(8,128)(2,1)} %bitcast.17), channel_id=1, source_target_pairs={{0,8},{1,9},{2,10},{3,11},{4,12},{5,13},{6,14},{7,15},{8,0},{9,1},... | collective-permute-start | bytes 1572872 | tf_op jit(solution)/shard_map/weight_half/ppermute | solution.py:39
  4.4 1.9 %collective-permute-start.8 = (bf16[256,1024]{1,0:T(8,128)(2,1)}, bf16[256,1024]{1,0:T(8,128)(2,1)}, u32[]{:S(2)}, u32[]{:S(2)}) collective-permute-start(bf16[256,1024]{1,0:T(8,128)(2,1)} %bitcast.50), channel_id=1, source_target_pairs={{0,16},{16,0},{32,48},{48,32},{64,80},{80,64},{96,112},{112,96},{1... | collective-permute-start | bytes 1572872 | tf_op jit(solution)/shard_map/island1/ppermute | solution.py:44
  7.2 2.4 %collective-permute-start.5 = (bf16[256,1024]{1,0:T(8,128)(2,1)}, bf16[256,1024]{1,0:T(8,128)(2,1)}, u32[]{:S(2)}, u32[]{:S(2)}) collective-permute-start(bf16[256,1024]{1,0:T(8,128)(2,1)} %bitcast.19), channel_id=1, source_target_pairs={{0,2},{1,3},{2,4},{3,5},{4,6},{5,7},{6,0},{7,1},{8,10},{9,11},{10,... | collective-permute-start | bytes 1572872 | tf_op jit(solution)/shard_map/weight_left/ppermute | solution.py:39
  10.3 3.5 %grad_near.1 = (bf16[256,1024]{1,0:T(8,128)(2,1)}, bf16[256,1024]{1,0:T(8,128)(2,1)S(1)}) custom-call(s32[16]{0:T(128)S(1)} %fusion.3.s, bf16[256,4096]{1,0:T(8,128)(2,1)} %bitcast.25, bf16[256,4096]{1,0:T(8,128)(2,1)S(1)} %collective-permute-done.refs_1_.refs_4_.refs_5_.refs_6_.refs_7_, bf16[256,1024]{1,0:T(8,128)(2,1)} %bitcast.40, ...), custom_call_target="tpu_custom_call" | custom-call | bytes 1000 | tf_op jit(solution)/shard_map/grad_near/pallas_call | solution.py:79
  14.9 2.8 %grad_far.1 = (bf16[256,1024]{1,0:T(8,128)(2,1)S(1)}, bf16[256,1024]{1,0:T(8,128)(2,1)S(1)}) custom-call(s32[16]{0:T(128)S(1)} %fusion.3.s, bf16[256,4096]{1,0:T(8,128)(2,1)} %bitcast.26, bf16[256,4096]{1,0:T(8,128)(2,1)S(1)} %collective-permute-done.refs_1_.refs_4_.refs_5_.refs_6_.refs_7_, bf16[256,1024]{1,0:T(8,128)(2,1)} %bitcast.41, ...), custom_call_target="tpu_custom_call" | custom-call | bytes 1000 | tf_op jit(solution)/shard_map/grad_far/pallas_call | solution.py:79
  19.0 2.1 %collective-permute-start.3 = (bf16[256,1024]{1,0:T(8,128)(2,1)}, bf16[256,1024]{1,0:T(8,128)(2,1)S(1)}, u32[]{:S(2)}, u32[]{:S(2)}) collective-permute-start(bf16[256,1024]{1,0:T(8,128)(2,1)} %collective-permute-done.2.refs_11_), channel_id=1, source_target_pairs={{0,2},{1,3},{2,4},{3,5},{4,6},{5,7},{6,0},{7,1},{8,10},{9,11},{10,... | collective-permute-start | bytes 1572872 | tf_op jit(solution)/shard_map/second_left/ppermute | solution.py:39
  22.4 3.3 %collective-permute-start.12 = (bf16[256,1024]{1,0:T(8,128)(2,1)S(1)}, bf16[256,1024]{1,0:T(8,128)(2,1)S(1)}, u32[]{:S(2)}, u32[]{:S(2)}) collective-permute-start(bf16[256,1024]{1,0:T(8,128)(2,1)S(1)} %copy-done.6), channel_id=1, source_target_pairs={{0,8},{1,9},{2,10},{3,11},{4,12},{5,13},{6,14},{7,15},{8,0},{9,1},... | collective-permute-start | bytes 1572872 | tf_op jit(solution)/shard_map/half_left/ppermute | solution.py:39
  25.7 4.5 %near.1 = (f32[256,1024]{1,0:T(8,128)S(1)}, f32[256,1024]{1,0:T(8,128)S(1)}, bf16[256,1024]{1,0:T(8,128)(2,1)S(1)}, bf16[256,1024]{1,0:T(8,128)(2,1)S(1)}) custom-call(s32[16]{0:T(128)S(1)} %fusion.3.s, bf16[256,4096]{1,0:T(8,128)(2,1)} %bitcast.27, bf16[256,4096]{1,0:T(8,128)(2,1)} %bitcast.28, bf16[256,4096]{1,0:T(8,128)(2,1)} %bitcast.29, ...), custom_call_target="tpu_custom_call" | custom-call | bytes 1000 | tf_op jit(solution)/shard_map/near/pallas_call | solution.py:79
  31.3 3.3 %collective-permute-start.11 = (f16[128,1024]{1,0:T(8,128)(2,1)S(1)}, f16[128,1024]{1,0:T(8,128)(2,1)S(1)}, u32[]{:S(2)}, u32[]{:S(2)}) collective-permute-start(f16[128,1024]{1,0:T(8,128)(2,1)S(1)} %get-tuple-element.67), channel_id=1, source_target_pairs={{0,32},{16,48},{32,0},{48,16},{64,96},{80,112},{96,64},{112,80},{1... | collective-permute-start | bytes 786440 | tf_op jit(solution)/shard_map/island2/ppermute | solution.py:44
  34.5 2.2 %add_right.1.refs_4_ = bf16[256,1024]{1,0:T(8,128)(2,1)S(1)} custom-call(s32[16]{0:T(128)S(1)} %fusion.3.s, bf16[256,4096]{1,0:T(8,128)(2,1)} %bitcast.31, bf16[256,4096]{1,0:T(8,128)(2,1)S(1)} %collective-permute-done.refs_1_.refs_4_.refs_5_.refs_6_.refs_7_, bf16[256,1024]{1,0:T(8,128)(2,1)} %bitcast.43, ...), custom_call_target="tpu_custom_call" | custom-call | bytes 1000 | tf_op jit(solution)/shard_map/add_right/pallas_call | solution.py:79
  38.3 1.6 %forward.1 = (bf16[256,1024]{1,0:T(8,128)(2,1)S(1)}, bf16[256,1024]{1,0:T(8,128)(2,1)S(1)}) custom-call(s32[16]{0:T(128)S(1)} %fusion.3.s, bf16[256,1024]{1,0:T(8,128)(2,1)} %collective-permute-done.5.refs_12_.refs_0_, bf16[256,1024]{1,0:T(8,128)(2,1)S(1)} %collective-permute-done.3.refs_1_.refs_10_, ...), custom_call_target="tpu_custom_call" | custom-call | bytes 1000 | tf_op jit(solution)/shard_map/forward/pallas_call | solution.py:79
  41.6 2.0 %collective-permute-start.9 = (bf16[256,1024]{1,0:T(8,128)(2,1)S(1)}, bf16[256,1024]{1,0:T(8,128)(2,1)S(1)}, u32[]{:S(2)}, u32[]{:S(2)}) collective-permute-start(bf16[256,1024]{1,0:T(8,128)(2,1)S(1)} %get-tuple-element.39.refs_6_), channel_id=1, source_target_pairs={{0,2},{1,3},{2,4},{3,5},{4,6},{5,7},{6,0},{7,1},{8,10},{9,11},{10,... | collective-permute-start | bytes 1572872 | tf_op jit(solution)/shard_map/third_left/ppermute | solution.py:39
  43.6 2.1 %add_left.1 = bf16[256,1024]{1,0:T(8,128)(2,1)S(1)} custom-call(s32[16]{0:T(128)S(1)} %fusion.3.s, bf16[256,4096]{1,0:T(8,128)(2,1)} %bitcast.32, bf16[256,4096]{1,0:T(8,128)(2,1)S(1)} %collective-permute-done.refs_1_.refs_4_.refs_5_.refs_6_.refs_7_, bf16[256,1024]{1,0:T(8,128)(2,1)} %bitcast.44, ...), custom_call_target="tpu_custom_call" | custom-call | bytes 1000 | tf_op jit(solution)/shard_map/add_left/pallas_call | solution.py:79
  46.5 5.9 %collective-permute-start.14 = (f16[128,1024]{1,0:T(8,128)(2,1)S(1)}, f16[128,1024]{1,0:T(8,128)(2,1)S(1)}, u32[]{:S(2)}, u32[]{:S(2)}) collective-permute-start(f16[128,1024]{1,0:T(8,128)(2,1)S(1)} %get-tuple-element.65), channel_id=1, source_target_pairs={{0,96},{16,112},{32,64},{48,80},{64,32},{80,48},{96,0},{112,16},{1... | collective-permute-start | bytes 786440 | tf_op jit(solution)/shard_map/island3/ppermute | solution.py:44
  52.4 3.0 %collective-permute-start.19 = (bf16[256,1024]{1,0:T(8,128)(2,1)S(1)}, bf16[256,1024]{1,0:T(8,128)(2,1)S(1)}, u32[]{:S(2)}, u32[]{:S(2)}) collective-permute-start(bf16[256,1024]{1,0:T(8,128)(2,1)S(1)} %get-tuple-element.51), channel_id=1, source_target_pairs={{0,8},{1,9},{2,10},{3,11},{4,12},{5,13},{6,14},{7,15},{8,0},{9,1},... | collective-permute-start | bytes 1572872 | tf_op jit(solution)/shard_map/half_own/ppermute | solution.py:39
  55.5 6.0 %collective-permute-done.9.refs_5_.refs_12_ = bf16[256,1024]{1,0:T(8,128)(2,1)S(1)} collective-permute-done((bf16[256,1024]{1,0:T(8,128)(2,1)S(1)}, bf16[256,1024]{1,0:T(8,128)(2,1)S(1)}, u32[]{:S(2)}, u32[]{:S(2)}) %collective-permute-start.9) | collective-permute-done | bytes 524320 | tf_op jit(solution)/shard_map/third_left/ppermute | solution.py:39
  61.5 2.1 %add_two.1 = bf16[256,1024]{1,0:T(8,128)(2,1)S(1)} custom-call(s32[16]{0:T(128)S(1)} %fusion.3.s, bf16[256,4096]{1,0:T(8,128)(2,1)} %bitcast.33, bf16[256,4096]{1,0:T(8,128)(2,1)S(1)} %collective-permute-done.refs_1_.refs_4_.refs_5_.refs_6_.refs_7_, bf16[256,1024]{1,0:T(8,128)(2,1)} %bitcast.45, ...), custom_call_target="tpu_custom_call" | custom-call | bytes 1000 | tf_op jit(solution)/shard_map/add_two/pallas_call | solution.py:79
  65.5 4.3 %far.1 = (f32[256,1024]{1,0:T(8,128)S(1)}, bf16[256,1024]{1,0:T(8,128)(2,1)S(1)}, bf16[256,1024]{1,0:T(8,128)(2,1)S(1)}, bf16[256,1024]{1,0:T(8,128)(2,1)S(1)}) custom-call(s32[16]{0:T(128)S(1)} %fusion.3.s, bf16[256,4096]{1,0:T(8,128)(2,1)} %bitcast.34, bf16[256,4096]{1,0:T(8,128)(2,1)} %bitcast.35, bf16[256,4096]{1,0:T(8,128)(2,1)} %bitcast.36, ...), custom_call_target="tpu_custom_call" | custom-call | bytes 1000 | tf_op jit(solution)/shard_map/far/pallas_call | solution.py:79
  70.4 8.6 %collective-permute-done.20.refs_6_ = bf16[256,1024]{1,0:T(8,128)(2,1)S(1)} collective-permute-done((bf16[256,1024]{1,0:T(8,128)(2,1)S(1)}, bf16[256,1024]{1,0:T(8,128)(2,1)S(1)}, u32[]{:S(2)}, u32[]{:S(2)}) %collective-permute-start.20) | collective-permute-done | bytes 524320 | tf_op jit(solution)/shard_map/along_left/ppermute | solution.py:39
  79.0 2.2 %add_own.1.refs_0_ = f32[256,1024]{1,0:T(8,128)S(1)} custom-call(s32[16]{0:T(128)S(1)} %fusion.3.s, bf16[256,4096]{1,0:T(8,128)(2,1)} %bitcast.38, bf16[256,4096]{1,0:T(8,128)(2,1)S(1)} %collective-permute-done.refs_1_.refs_4_.refs_5_.refs_6_.refs_7_, bf16[256,1024]{1,0:T(8,128)(2,1)} %bitcast.47, ...), custom_call_target="tpu_custom_call" | custom-call | bytes 1000 | tf_op jit(solution)/shard_map/add_own/pallas_call | solution.py:79
  81.6 2.0 %collective-permute-start.23 = (f16[128,1024]{1,0:T(8,128)(2,1)S(1)}, f16[128,1024]{1,0:T(8,128)(2,1)S(1)}, u32[]{:S(2)}, u32[]{:S(2)}) collective-permute-start(f16[128,1024]{1,0:T(8,128)(2,1)S(1)} %get-tuple-element.61), channel_id=1, source_target_pairs={{0,16},{16,0},{32,48},{48,32},{64,80},{80,64},{96,112},{112,96},{1... | collective-permute-start | bytes 786440 | tf_op jit(solution)/shard_map/island5/ppermute | solution.py:44
  83.6 2.7 %adam.1 = (bf16[256,1024]{1,0:T(8,128)(2,1)}, f32[256,1024]{1,0:T(8,128)}, f32[256,1024]{1,0:T(8,128)}) custom-call(s32[16]{0:T(128)S(1)} %fusion.3.s, f32[256,1024]{1,0:T(8,128)S(1)} %add_own.1.refs_0_, bf16[256,1024]{1,0:T(8,128)(2,1)S(1)} %collective-permute-done.21.refs_1_, bf16[256,1024]{1,0:T(8,128)(2,1)S(1)} %bitcast.21, f32[256,1024]{1,0:T(8,128)S(1)} %bitcast.22, ...), custom_call_target="tpu_custom_call" | custom-call | bytes 1000 | tf_op jit(solution)/shard_map/adam/pallas_call | solution.py:79
  86.3 2.4 %finish.1 = (bf16[256,1024]{1,0:T(8,128)(2,1)}, bf16[256,4096]{1,0:T(8,128)(2,1)}) custom-call(s32[16]{0:T(128)S(1)} %fusion.3.s, f32[256,1024]{1,0:T(8,128)S(1)} %get-tuple-element.46.refs_7_.refs_0_, bf16[256,1024]{1,0:T(8,128)(2,1)S(1)} %get-tuple-element.47.refs_1_, bf16[256,1024]{1,0:T(8,128)(2,1)S(1)} %get-tuple-element.48.refs_2_, ...), custom_call_target="tpu_custom_call" | custom-call | bytes 1000 | tf_op jit(solution)/shard_map/finish/pallas_call | solution.py:79
  88.8 2.0 %merge.1 = (f32[256,1024]{1,0:T(8,128)}, f32[256,1024]{1,0:T(8,128)}) custom-call(s32[16]{0:T(128)S(1)} %fusion.3.s, f32[128,1024]{1,0:T(8,128)S(1)} %get-tuple-element.62.refs_5_.refs_0_, f32[128,1024]{1,0:T(8,128)S(1)} %convert_element_type.43.refs_1_, f32[256,1024]{1,0:T(8,128)S(1)} %copy-done, f32[256,1024]{1,0:T(8,128)S(1)} %copy-done.4, ...), custom_call_target="tpu_custom_call" | custom-call | bytes 1000 | tf_op jit(solution)/shard_map/merge/pallas_call | solution.py:79
  (58 shorter events, 13.6 us)
Async XLA Ops:
  0.6 9.6 %collective-permute-start = (bf16[256,4096]{1,0:T(8,128)(2,1)}, bf16[256,4096]{1,0:T(8,128)(2,1)S(1)}, u32[]{:S(2)}, u32[]{:S(2)}) collective-permute-start(bf16[256,4096]{1,0:T(8,128)(2,1)} %bitcast.24), channel_id=1, source_target_pairs={{0,1},{1,0},{2,3},{3,2},{4,5},{5,4},{6,7},{7,6},{8,9},{9,8},{10,11... | collective-permute-start | bytes 6291464 | tf_op jit(solution)/shard_map/peer_hidden/ppermute | solution.py:39
  0.7 6.4 %collective-permute-start.1 = (bf16[256,1024]{1,0:T(8,128)(2,1)}, bf16[256,1024]{1,0:T(8,128)(2,1)S(1)}, u32[]{:S(2)}, u32[]{:S(2)}) collective-permute-start(bf16[256,1024]{1,0:T(8,128)(2,1)} %bitcast.39), channel_id=1, source_target_pairs={{0,1},{1,0},{2,3},{3,2},{4,5},{5,4},{6,7},{7,6},{8,9},{9,8},{10,11... | collective-permute-start | bytes 1572872 | tf_op jit(solution)/shard_map/peer_cotangent/ppermute | solution.py:39
  1.2 16.5 %collective-permute-start.2 = (bf16[256,1024]{1,0:T(8,128)(2,1)}, bf16[256,1024]{1,0:T(8,128)(2,1)}, u32[]{:S(2)}, u32[]{:S(2)}) collective-permute-start(bf16[256,1024]{1,0:T(8,128)(2,1)} %bitcast.17), channel_id=1, source_target_pairs={{0,8},{1,9},{2,10},{3,11},{4,12},{5,13},{6,14},{7,15},{8,0},{9,1},... | collective-permute-start | bytes 1572872 | tf_op jit(solution)/shard_map/weight_half/ppermute | solution.py:39
  4.4 14.6 %collective-permute-start.8 = (bf16[256,1024]{1,0:T(8,128)(2,1)}, bf16[256,1024]{1,0:T(8,128)(2,1)}, u32[]{:S(2)}, u32[]{:S(2)}) collective-permute-start(bf16[256,1024]{1,0:T(8,128)(2,1)} %bitcast.50), channel_id=1, source_target_pairs={{0,16},{16,0},{32,48},{48,32},{64,80},{80,64},{96,112},{112,96},{1... | collective-permute-start | bytes 1572872 | tf_op jit(solution)/shard_map/island1/ppermute | solution.py:44
  6.3 16.1 %collective-permute-start.6 = (bf16[256,1024]{1,0:T(8,128)(2,1)}, bf16[256,1024]{1,0:T(8,128)(2,1)S(1)}, u32[]{:S(2)}, u32[]{:S(2)}) collective-permute-start(bf16[256,1024]{1,0:T(8,128)(2,1)} %bitcast.18), channel_id=1, source_target_pairs={{0,6},{1,7},{2,0},{3,1},{4,2},{5,3},{6,4},{7,5},{8,14},{9,15},{10,... | collective-permute-start | bytes 1572872 | tf_op jit(solution)/shard_map/weight_right/ppermute | solution.py:39
  7.2 18.5 %collective-permute-start.5 = (bf16[256,1024]{1,0:T(8,128)(2,1)}, bf16[256,1024]{1,0:T(8,128)(2,1)}, u32[]{:S(2)}, u32[]{:S(2)}) collective-permute-start(bf16[256,1024]{1,0:T(8,128)(2,1)} %bitcast.19), channel_id=1, source_target_pairs={{0,2},{1,3},{2,4},{3,5},{4,6},{5,7},{6,0},{7,1},{8,10},{9,11},{10,... | collective-permute-start | bytes 1572872 | tf_op jit(solution)/shard_map/weight_left/ppermute | solution.py:39
  14.6 16.7 %collective-permute-start.7 = (bf16[256,1024]{1,0:T(8,128)(2,1)}, bf16[256,1024]{1,0:T(8,128)(2,1)}, u32[]{:S(2)}, u32[]{:S(2)}) collective-permute-start(bf16[256,1024]{1,0:T(8,128)(2,1)} %get-tuple-element.34.refs_4_), channel_id=1, source_target_pairs={{0,8},{1,9},{2,10},{3,11},{4,12},{5,13},{6,14},{7,15},{8,0},{9,1},... | collective-permute-start | bytes 1572872 | tf_op jit(solution)/shard_map/half_right/ppermute | solution.py:39
  17.8 19.0 %collective-permute-start.4 = (bf16[256,1024]{1,0:T(8,128)(2,1)}, bf16[256,1024]{1,0:T(8,128)(2,1)S(1)}, u32[]{:S(2)}, u32[]{:S(2)}) collective-permute-start(bf16[256,1024]{1,0:T(8,128)(2,1)} %collective-permute-done.2.refs_11_), channel_id=1, source_target_pairs={{0,6},{1,7},{2,0},{3,1},{4,2},{5,3},{6,4},{7,5},{8,14},{9,15},{10,... | collective-permute-start | bytes 1572872 | tf_op jit(solution)/shard_map/second_right/ppermute | solution.py:39
  19.0 18.9 %collective-permute-start.3 = (bf16[256,1024]{1,0:T(8,128)(2,1)}, bf16[256,1024]{1,0:T(8,128)(2,1)S(1)}, u32[]{:S(2)}, u32[]{:S(2)}) collective-permute-start(bf16[256,1024]{1,0:T(8,128)(2,1)} %collective-permute-done.2.refs_11_), channel_id=1, source_target_pairs={{0,2},{1,3},{2,4},{3,5},{4,6},{5,7},{6,0},{7,1},{8,10},{9,11},{10,... | collective-permute-start | bytes 1572872 | tf_op jit(solution)/shard_map/second_left/ppermute | solution.py:39
  22.4 17.9 %collective-permute-start.12 = (bf16[256,1024]{1,0:T(8,128)(2,1)S(1)}, bf16[256,1024]{1,0:T(8,128)(2,1)S(1)}, u32[]{:S(2)}, u32[]{:S(2)}) collective-permute-start(bf16[256,1024]{1,0:T(8,128)(2,1)S(1)} %copy-done.6), channel_id=1, source_target_pairs={{0,8},{1,9},{2,10},{3,11},{4,12},{5,13},{6,14},{7,15},{8,0},{9,1},... | collective-permute-start | bytes 1572872 | tf_op jit(solution)/shard_map/half_left/ppermute | solution.py:39
  30.2 11.3 %collective-permute-start.13 = (bf16[256,1024]{1,0:T(8,128)(2,1)S(1)}, bf16[256,1024]{1,0:T(8,128)(2,1)S(1)}, u32[]{:S(2)}, u32[]{:S(2)}) collective-permute-start(bf16[256,1024]{1,0:T(8,128)(2,1)S(1)} %get-tuple-element.43), channel_id=1, source_target_pairs={{0,1},{1,0},{2,3},{3,2},{4,5},{5,4},{6,7},{7,6},{8,9},{9,8},{10,11... | collective-permute-start | bytes 1572872 | tf_op jit(solution)/shard_map/got_near/ppermute | solution.py:39
  31.3 14.9 %collective-permute-start.11 = (f16[128,1024]{1,0:T(8,128)(2,1)S(1)}, f16[128,1024]{1,0:T(8,128)(2,1)S(1)}, u32[]{:S(2)}, u32[]{:S(2)}) collective-permute-start(f16[128,1024]{1,0:T(8,128)(2,1)S(1)} %get-tuple-element.67), channel_id=1, source_target_pairs={{0,32},{16,48},{32,0},{48,16},{64,96},{80,112},{96,64},{112,80},{1... | collective-permute-start | bytes 786440 | tf_op jit(solution)/shard_map/island2/ppermute | solution.py:44
  36.8 15.6 %collective-permute-start.15 = (bf16[256,1024]{1,0:T(8,128)(2,1)S(1)}, bf16[256,1024]{1,0:T(8,128)(2,1)S(1)}, u32[]{:S(2)}, u32[]{:S(2)}) collective-permute-start(bf16[256,1024]{1,0:T(8,128)(2,1)S(1)} %get-tuple-element.35), channel_id=1, source_target_pairs={{0,8},{1,9},{2,10},{3,11},{4,12},{5,13},{6,14},{7,15},{8,0},{9,1},... | collective-permute-start | bytes 1572872 | tf_op jit(solution)/shard_map/half_two/ppermute | solution.py:39
  37.9 23.6 %collective-permute-start.16 = (bf16[256,1024]{1,0:T(8,128)(2,1)S(1)}, bf16[256,1024]{1,0:T(8,128)(2,1)S(1)}, u32[]{:S(2)}, u32[]{:S(2)}) collective-permute-start(bf16[256,1024]{1,0:T(8,128)(2,1)S(1)} %add_right.1.refs_4_), channel_id=1, source_target_pairs={{0,2},{1,3},{2,4},{3,5},{4,6},{5,7},{6,0},{7,1},{8,10},{9,11},{10,... | collective-permute-start | bytes 1572872 | tf_op jit(solution)/shard_map/along_right/ppermute | solution.py:39
  40.4 15.1 %collective-permute-start.10 = (bf16[256,1024]{1,0:T(8,128)(2,1)S(1)}, bf16[256,1024]{1,0:T(8,128)(2,1)S(1)}, u32[]{:S(2)}, u32[]{:S(2)}) collective-permute-start(bf16[256,1024]{1,0:T(8,128)(2,1)S(1)} %get-tuple-element.40), channel_id=1, source_target_pairs={{0,6},{1,7},{2,0},{3,1},{4,2},{5,3},{6,4},{7,5},{8,14},{9,15},{10,... | collective-permute-start | bytes 1572872 | tf_op jit(solution)/shard_map/third_right/ppermute | solution.py:39
  41.6 20.0 %collective-permute-start.9 = (bf16[256,1024]{1,0:T(8,128)(2,1)S(1)}, bf16[256,1024]{1,0:T(8,128)(2,1)S(1)}, u32[]{:S(2)}, u32[]{:S(2)}) collective-permute-start(bf16[256,1024]{1,0:T(8,128)(2,1)S(1)} %get-tuple-element.39.refs_6_), channel_id=1, source_target_pairs={{0,2},{1,3},{2,4},{3,5},{4,6},{5,7},{6,0},{7,1},{8,10},{9,11},{10,... | collective-permute-start | bytes 1572872 | tf_op jit(solution)/shard_map/third_left/ppermute | solution.py:39
  46.5 17.1 %collective-permute-start.14 = (f16[128,1024]{1,0:T(8,128)(2,1)S(1)}, f16[128,1024]{1,0:T(8,128)(2,1)S(1)}, u32[]{:S(2)}, u32[]{:S(2)}) collective-permute-start(f16[128,1024]{1,0:T(8,128)(2,1)S(1)} %get-tuple-element.65), channel_id=1, source_target_pairs={{0,96},{16,112},{32,64},{48,80},{64,32},{80,48},{96,0},{112,16},{1... | collective-permute-start | bytes 786440 | tf_op jit(solution)/shard_map/island3/ppermute | solution.py:44
  52.4 17.5 %collective-permute-start.19 = (bf16[256,1024]{1,0:T(8,128)(2,1)S(1)}, bf16[256,1024]{1,0:T(8,128)(2,1)S(1)}, u32[]{:S(2)}, u32[]{:S(2)}) collective-permute-start(bf16[256,1024]{1,0:T(8,128)(2,1)S(1)} %get-tuple-element.51), channel_id=1, source_target_pairs={{0,8},{1,9},{2,10},{3,11},{4,12},{5,13},{6,14},{7,15},{8,0},{9,1},... | collective-permute-start | bytes 1572872 | tf_op jit(solution)/shard_map/half_own/ppermute | solution.py:39
  55.5 23.6 %collective-permute-start.20 = (bf16[256,1024]{1,0:T(8,128)(2,1)S(1)}, bf16[256,1024]{1,0:T(8,128)(2,1)S(1)}, u32[]{:S(2)}, u32[]{:S(2)}) collective-permute-start(bf16[256,1024]{1,0:T(8,128)(2,1)S(1)} %add_left.1), channel_id=1, source_target_pairs={{0,6},{1,7},{2,0},{3,1},{4,2},{5,3},{6,4},{7,5},{8,14},{9,15},{10,... | collective-permute-start | bytes 1572872 | tf_op jit(solution)/shard_map/along_left/ppermute | solution.py:39
  64.0 17.3 %collective-permute-start.22 = (f16[128,1024]{1,0:T(8,128)(2,1)S(1)}, f16[128,1024]{1,0:T(8,128)(2,1)S(1)}, u32[]{:S(2)}, u32[]{:S(2)}) collective-permute-start(f16[128,1024]{1,0:T(8,128)(2,1)S(1)} %get-tuple-element.63), channel_id=1, source_target_pairs={{0,128},{16,144},{32,160},{48,176},{64,192},{80,208},{96,224},{112... | collective-permute-start | bytes 786440 | tf_op jit(solution)/shard_map/island4/ppermute | solution.py:44
  65.4 18.2 %collective-permute-start.21 = (bf16[256,1024]{1,0:T(8,128)(2,1)S(1)}, bf16[256,1024]{1,0:T(8,128)(2,1)S(1)}, u32[]{:S(2)}, u32[]{:S(2)}) collective-permute-start(bf16[256,1024]{1,0:T(8,128)(2,1)S(1)} %add_two.1), channel_id=1, source_target_pairs={{0,4},{1,5},{2,6},{3,7},{4,0},{5,1},{6,2},{7,3},{8,12},{9,13},{10,... | collective-permute-start | bytes 1572872 | tf_op jit(solution)/shard_map/along_two/ppermute | solution.py:39
  69.8 16.5 %collective-permute-start.17 = (bf16[256,1024]{1,0:T(8,128)(2,1)S(1)}, bf16[256,1024]{1,0:T(8,128)(2,1)S(1)}, u32[]{:S(2)}, u32[]{:S(2)}) collective-permute-start(bf16[256,1024]{1,0:T(8,128)(2,1)S(1)} %get-tuple-element.49), channel_id=1, source_target_pairs={{0,1},{1,0},{2,3},{3,2},{4,5},{5,4},{6,7},{7,6},{8,9},{9,8},{10,11... | collective-permute-start | bytes 1572872 | tf_op jit(solution)/shard_map/got_far/ppermute | solution.py:39
  69.9 16.4 %collective-permute-start.18 = (bf16[256,1024]{1,0:T(8,128)(2,1)S(1)}, bf16[256,1024]{1,0:T(8,128)(2,1)S(1)}, u32[]{:S(2)}, u32[]{:S(2)}) collective-permute-start(bf16[256,1024]{1,0:T(8,128)(2,1)S(1)} %get-tuple-element.50), channel_id=1, source_target_pairs={{0,1},{1,0},{2,3},{3,2},{4,5},{5,4},{6,7},{7,6},{8,9},{9,8},{10,11... | collective-permute-start | bytes 1572872 | tf_op jit(solution)/shard_map/got_terms/ppermute | solution.py:39
  81.6 7.1 %collective-permute-start.23 = (f16[128,1024]{1,0:T(8,128)(2,1)S(1)}, f16[128,1024]{1,0:T(8,128)(2,1)S(1)}, u32[]{:S(2)}, u32[]{:S(2)}) collective-permute-start(f16[128,1024]{1,0:T(8,128)(2,1)S(1)} %get-tuple-element.61), channel_id=1, source_target_pairs={{0,16},{16,0},{32,48},{48,32},{64,80},{80,64},{96,112},{112,96},{1... | collective-permute-start | bytes 786440 | tf_op jit(solution)/shard_map/island5/ppermute | solution.py:44
  (8 other events, 37.9 us)
